TPU v7x, 256 devices: a whole 4x4x8 slice. The times are simulated.
256 devices in a mesh: dp: 32 (over x, y, core), ctx: 8 (over z).
Axes of the slice: x: 4, y: 4, z: 8, core: 2. Of those that a mesh axis runs over, the one named last changes fastest.
Arguments:
- queries: bfloat16 [32, 2048, 1024], P('dp', 'ctx'), may hold values from -6 to 6
- keys: bfloat16 [32, 2048, 1024], P('dp', 'ctx'), may hold values from -6 to 6
- values: bfloat16 [32, 2048, 1024], P('dp', 'ctx'), may hold values from -6 to 6
- gates: bfloat16 [32, 2048, 1024], P('dp', 'ctx'), may hold values from -6 to 6
- cotangent: bfloat16 [32, 2048, 1024], P('dp', 'ctx'), may hold values from -6 to 6
- out_weight: bfloat16 [1024, 1024], replicated, may hold values from -0.1875 to 0.1875
- position_bias: float32 [8, 128], replicated, may hold values from -4 to 4
- distance_bucket: int32 [768], replicated, may hold values from 0 to 127, as said below
- history_lengths: int32 [32, 8], P('dp'), may hold values from 0 to 768, as said below
- first_device: int32 [32], P('dp'), may hold values from 0 to 7
Outputs:
- d_queries: bfloat16 [32, 2048, 1024], P('dp', 'ctx')
- d_keys: bfloat16 [32, 2048, 1024], P('dp', 'ctx')
- d_values: bfloat16 [32, 2048, 1024], P('dp', 'ctx')
- d_gates: bfloat16 [32, 2048, 1024], P('dp', 'ctx')
- d_out_weight: float32 [1024, 1024], P('dp', 'ctx')
Inputs may be any that keep to these rules, and one draw needn't show every extreme that they name: `distance_bucket`: Non-decreasing in the distance, 0 at distance 0, rising by at most 1 from one distance to the next. `history_lengths`: in each group the users' block counts ceil(length / 256) are 1 to 3 and sum to 8; entries after the last user are 0; every group has a user of exactly 768 events.
All inputs are finite; a program needn't handle non-finite values.
Results may differ from a plain program's by a relative error of at most 0.025.
Values may be sent and summed in bfloat16 or wider, within the bound.
A program may use at most 128 MiB of HBM per device.

v0:
```python
import jax
import jax.numpy as jnp
from jax import lax
from jax.sharding import PartitionSpec as P

MAXB = 3


epsilon = 1e-05


def passed_along(block, axis, distance):
    devices = range(lax.axis_size(axis))
    route = [((i - distance) % len(devices), i) for i in devices]
    return lax.ppermute(block, axis, route)


def block_place(lengths_row, logical_block, block_rows):
    slot_count = lengths_row.shape[0]
    blocks_per = (lengths_row + block_rows - 1) // block_rows
    block_ends = jnp.cumsum(blocks_per)
    owner = jnp.sum((block_ends <= logical_block).astype(jnp.int32))
    chosen = jnp.arange(slot_count, dtype=jnp.int32) == owner
    user_len = jnp.sum(jnp.where(chosen, lengths_row, 0))
    user_end = jnp.sum(jnp.where(chosen, block_ends, 0))
    user_blocks = jnp.sum(jnp.where(chosen, blocks_per, 0))
    return (logical_block - (user_end - user_blocks), user_len)


def make_mask(offset, inner_block, user_len, block_rows):
    row_index = jnp.arange(block_rows, dtype=jnp.int32)
    query_live = inner_block * block_rows + row_index < user_len
    key_live = ((inner_block - offset) * block_rows + row_index < user_len) & (
        offset <= inner_block
    )
    pair_mask = query_live[:, None] & key_live[None, :]
    if offset == 0:
        pair_mask = pair_mask & (row_index[None, :] <= row_index[:, None])
    return pair_mask


def make_table(position_bias, distance_bucket):
    bucket_count = position_bias.shape[1]
    one_hot = (
        distance_bucket[:, None] == jnp.arange(bucket_count, dtype=jnp.int32)[None, :]
    ).astype(jnp.float32)
    return lax.dot_general(
        position_bias, one_hot, (((1,), (1,)), ((), ())), precision=lax.Precision.HIGHEST
    )


def toeplitz_bias(bias_dist, offset, block_rows):
    head_count = bias_dist.shape[0]
    padded = jnp.pad(bias_dist, ((0, 0), (block_rows - 1, 1)))
    window = padded[:, offset * block_rows : offset * block_rows + 2 * block_rows - 1]
    folded = jnp.concatenate(
        [
            jnp.flip(window[:, :block_rows], 1),
            jnp.zeros((head_count, 1), jnp.float32),
            jnp.flip(window[:, block_rows:], 1),
        ],
        1,
    )
    tiled = jnp.broadcast_to(folded[:, None, :], (head_count, block_rows, 2 * block_rows)).reshape(
        head_count, 2 * block_rows * block_rows
    )
    sheared = tiled[:, : block_rows * (2 * block_rows - 1)].reshape(
        head_count, block_rows, 2 * block_rows - 1
    )
    return sheared[:, :, :block_rows]


def on_device(
    queries,
    keys,
    values,
    gates,
    cotangent,
    out_weight,
    position_bias,
    distance_bucket,
    history_lengths,
    first_device,
):
    query_rows = queries[0]
    block_rows, model_width = query_rows.shape
    head_count = position_bias.shape[0]
    head_dim = model_width // head_count
    score_scale = head_dim ** (-0.5)
    ctx_count = lax.axis_size("ctx")
    logical_block = jnp.mod(lax.axis_index("ctx") - first_device[0], ctx_count)
    inner_block, user_len = block_place(history_lengths[0], logical_block, block_rows)
    bias_dist = make_table(position_bias, distance_bucket)
    own_pair = jnp.stack([keys[0], values[0]])
    pair_blocks = [own_pair]
    for offset in range(1, MAXB):
        pair_blocks.append(passed_along(own_pair, "ctx", offset))
    query_heads = query_rows.reshape(block_rows, head_count, head_dim)
    row_index = jnp.arange(block_rows, dtype=jnp.int32)
    mixed_out = jnp.zeros((block_rows, model_width), jnp.float32)
    for offset in range(MAXB):
        key_heads = pair_blocks[offset][0].reshape(block_rows, head_count, head_dim)
        value_heads = pair_blocks[offset][1].reshape(block_rows, head_count, head_dim)
        pair_bias = toeplitz_bias(bias_dist, offset, block_rows)
        pair_mask = make_mask(offset, inner_block, user_len, block_rows)
        score = (
            score_scale
            * jnp.einsum("rhe,che->hrc", query_heads, key_heads, preferred_element_type=jnp.float32)
            + pair_bias
        )
        weight = jnp.where(pair_mask[None], jax.nn.silu(score), 0.0).astype(jnp.bfloat16)
        mixed_out = mixed_out + jnp.einsum(
            "hrc,che->rhe", weight, value_heads, preferred_element_type=jnp.float32
        ).reshape(block_rows, model_width)
    centered = mixed_out - jnp.mean(mixed_out, axis=1, keepdims=True)
    inverse = lax.rsqrt(jnp.mean(centered * centered, axis=1, keepdims=True) + epsilon)
    normed = centered * inverse
    live = (inner_block * block_rows + row_index < user_len)[:, None]
    gate_float = gates[0].astype(jnp.float32)
    gated_rows = jnp.where(live, normed * gate_float, 0.0).astype(jnp.bfloat16)
    grad_out = cotangent[0]
    d_gated = lax.dot_general(
        grad_out, out_weight, (((1,), (1,)), ((), ())), preferred_element_type=jnp.float32
    )
    d_gates = jnp.where(live, d_gated * normed, 0.0).astype(jnp.bfloat16)
    d_normed = jnp.where(live, d_gated * gate_float, 0.0)
    d_mixed = inverse * (
        d_normed
        - jnp.mean(d_normed, axis=1, keepdims=True)
        - normed * jnp.mean(d_normed * normed, axis=1, keepdims=True)
    )
    d_mixed_heads = d_mixed.astype(jnp.bfloat16).reshape(block_rows, head_count, head_dim)
    d_query = jnp.zeros((block_rows, head_count, head_dim), jnp.float32)
    key_parts = []
    for offset in range(MAXB):
        key_heads = pair_blocks[offset][0].reshape(block_rows, head_count, head_dim)
        value_heads = pair_blocks[offset][1].reshape(block_rows, head_count, head_dim)
        pair_bias = toeplitz_bias(bias_dist, offset, block_rows)
        pair_mask = make_mask(offset, inner_block, user_len, block_rows)
        score = (
            score_scale
            * jnp.einsum("rhe,che->hrc", query_heads, key_heads, preferred_element_type=jnp.float32)
            + pair_bias
        )
        weight = jnp.where(pair_mask[None], jax.nn.silu(score), 0.0).astype(jnp.bfloat16)
        d_attn = jnp.einsum(
            "rhe,che->hrc", d_mixed_heads, value_heads, preferred_element_type=jnp.float32
        )
        sigmoid_score = jax.nn.sigmoid(score)
        d_score = jnp.where(
            pair_mask[None], d_attn * sigmoid_score * (1.0 + score * (1.0 - sigmoid_score)), 0.0
        ).astype(jnp.bfloat16)
        d_query = d_query + jnp.einsum(
            "hrc,che->rhe", d_score, key_heads, preferred_element_type=jnp.float32
        )
        d_key = score_scale * jnp.einsum(
            "hrc,rhe->che", d_score, query_heads, preferred_element_type=jnp.float32
        )
        d_value = jnp.einsum(
            "hrc,rhe->che", weight, d_mixed_heads, preferred_element_type=jnp.float32
        )
        key_parts.append(
            jnp.stack(
                [d_key.reshape(block_rows, model_width), d_value.reshape(block_rows, model_width)]
            )
        )
    key_total = key_parts[0]
    for offset in range(1, MAXB):
        key_total = key_total + passed_along(
            key_parts[offset].astype(jnp.bfloat16), "ctx", -offset
        ).astype(jnp.float32)
    weight_terms = lax.dot_general(
        gated_rows, grad_out, (((0,), (0,)), ((), ())), preferred_element_type=jnp.float32
    )
    shared_terms = lax.psum_scatter(
        weight_terms.astype(jnp.bfloat16), "ctx", scatter_dimension=1, tiled=True
    )
    d_out_weight = lax.psum_scatter(shared_terms, "dp", scatter_dimension=0, tiled=True).astype(
        jnp.float32
    )
    d_queries = (score_scale * d_query).reshape(block_rows, model_width).astype(jnp.bfloat16)
    d_keys = key_total[0].astype(jnp.bfloat16)
    d_values = key_total[1].astype(jnp.bfloat16)
    return (d_queries[None], d_keys[None], d_values[None], d_gates[None], d_out_weight)


def solution(mesh):
    return jax.shard_map(
        on_device,
        mesh=mesh,
        in_specs=(
            P("dp", "ctx", None),
            P("dp", "ctx", None),
            P("dp", "ctx", None),
            P("dp", "ctx", None),
            P("dp", "ctx", None),
            P(),
            P(),
            P(),
            P("dp", None),
            P("dp"),
        ),
        out_specs=(
            P("dp", "ctx", None),
            P("dp", "ctx", None),
            P("dp", "ctx", None),
            P("dp", "ctx", None),
            P("dp", "ctx"),
        ),
        check_vma=False,
    )
```

profile of v0, /device:TPU:32, one launch (start us, length us, event | category | flops | bytes accessed | tf_op | source)
XLA Modules:
  0.0 263.4 jit_solution(2846840910463901023)
XLA Ops:
  11.2 3.3 %collective-permute-start.1 = (bf16[2,256,1024]{1,2,0:T(8,128)(2,1)}, bf16[2,256,1024]{1,2,0:T(8,128)(2,1)}, u32[]{:S(2)}, u32[]{:S(2)}) collective-permute-start(bf16[2,256,1024]{1,2,0:T(8,128)(2,1)} %pad_maximum_fusion), channel_id=1, source_target_pairs={{6,0},{7,1},{0,2},{1,3},{2,4},{3,5},{4,6},{5,7},{14,8},{15,9},{8,1... | collective-permute-start | bytes 3145736 | tf_op jit(solution)/shard_map/ppermute | solution.py:15
  14.4 3.1 %collective-permute-start = (bf16[2,256,1024]{1,2,0:T(8,128)(2,1)}, bf16[2,256,1024]{1,2,0:T(8,128)(2,1)}, u32[]{:S(2)}, u32[]{:S(2)}) collective-permute-start(bf16[2,256,1024]{1,2,0:T(8,128)(2,1)} %pad_maximum_fusion), channel_id=1, source_target_pairs={{7,0},{0,1},{1,2},{2,3},{3,4},{4,5},{5,6},{6,7},{15,8},{8,9},{9,10... | collective-permute-start | bytes 3145736 | tf_op jit(solution)/shard_map/ppermute | solution.py:15
  26.8 2.1 copy.128
  28.9 2.3 copy.115
  31.7 2.2 slice.118
  33.9 8.0 %reshape.304 = f32[8,256,511]{2,1,0:T(8,128)} reshape(f32[8,130816]{1,0:T(8,128)} %slice.118) | data formatting | bytes 8372224 | tf_op jit(solution)/shard_map/reshape | solution.py:67
  42.4 2.2 slice.112
  44.6 7.9 %reshape.302 = f32[8,256,511]{2,1,0:T(8,128)} reshape(f32[8,130816]{1,0:T(8,128)} %slice.112) | data formatting | bytes 8372224 | tf_op jit(solution)/shard_map/reshape | solution.py:67
  53.0 2.2 slice.106
  55.3 7.9 %reshape.300 = f32[8,256,511]{2,1,0:T(8,128)} reshape(f32[8,130816]{1,0:T(8,128)} %slice.106) | data formatting | bytes 8372224 | tf_op jit(solution)/shard_map/reshape | solution.py:67
  63.4 4.0 %select_convert_fusion.5 = (bf16[8,256,256]{2,1,0:T(8,128)(2,1)S(1)}, f32[8,256,256]{2,1,0:T(8,128)}) fusion(pred[256,256]{1,0:T(8,128)(4,1)S(1)} %get-tuple-element.45, f32[8,256,511]{2,1,0:T(8,128)} %reshape.300, bf16[256,8,128]{0,2,1:T(8,128)(2,1)S(1)} %bitcast.154, bf16[256,8,128]{0,2,1:T(8,128)(2,1)S(1)} %bitcast.166), kind=kOutput, calls=%fused_computation.13 | convolution fusion | flops 138412032 | bytes 6356992 | tf_op jit(solution)/shard_map/rhe,che->hrc/dot_general | solution.py:108
  67.9 1.9 fusion.24
  70.3 2.3 select_convert_fusion.3
  72.6 10.2 %collective-permute-done = bf16[2,256,1024]{1,2,0:T(8,128)(2,1)} collective-permute-done((bf16[2,256,1024]{1,2,0:T(8,128)(2,1)}, bf16[2,256,1024]{1,2,0:T(8,128)(2,1)}, u32[]{:S(2)}, u32[]{:S(2)}) %collective-permute-start) | collective-permute-done | bytes 1048608 | tf_op jit(solution)/shard_map/ppermute | solution.py:15
  84.1 2.2 select_convert_fusion.4
  88.9 2.3 select_convert_fusion.6
  93.8 1.8 convolution_convert_fusion
  95.6 2.6 copy.123
  103.2 2.7 %select_convert_fusion.1 = bf16[8,256,256]{2,1,0:T(8,128)(2,1)S(1)} fusion(f32[8,256,256]{2,1,0:T(8,128)} %get-tuple-element.49, bf16[256,8,128]{0,2,1:T(8,128)(2,1)S(1)} %bitcast.162, bf16[256,8,128]{0,2,1:T(8,128)(2,1)S(1)} %bitcast.177, pred[256,256]{1,0:T(8,128)(4,1)S(1)} %get-tuple-element.44), kind=kOutput, calls=%fused_computation.7 | convolution fusion | flops 139460608 | bytes 4259840 | tf_op jit(solution)/shard_map/rhe,che->hrc/dot_general | solution.py:146
  107.2 2.8 %select_convert_fusion = bf16[8,256,256]{2,1,0:T(8,128)(2,1)S(1)} fusion(f32[8,256,256]{2,1,0:T(8,128)} %get-tuple-element.51, bf16[256,8,128]{0,2,1:T(8,128)(2,1)S(1)} %bitcast.163, bf16[256,8,128]{0,2,1:T(8,128)(2,1)} %bitcast.187, pred[256,256]{1,0:T(8,128)(4,1)S(1)} %get-tuple-element.43), kind=kOutput, calls=%fused_computation.6 | convolution fusion | flops 139460608 | bytes 4259840 | tf_op jit(solution)/shard_map/rhe,che->hrc/dot_general | solution.py:146
  112.3 2.1 copy.113
  114.3 2.3 pad_maximum_fusion.2
  116.6 3.3 %collective-permute-start.3 = (bf16[2,256,1024]{2,1,0:T(8,128)(2,1)}, bf16[2,256,1024]{2,1,0:T(8,128)(2,1)}, u32[]{:S(2)}, u32[]{:S(2)}) collective-permute-start(bf16[2,256,1024]{2,1,0:T(8,128)(2,1)} %pad_maximum_fusion.2), channel_id=1, source_target_pairs={{2,0},{3,1},{4,2},{5,3},{6,4},{7,5},{0,6},{1,7},{10,8},{11,9},{12,... | collective-permute-start | bytes 3145736 | tf_op jit(solution)/shard_map/ppermute | solution.py:15
  120.9 2.2 collective-permute-start.2
  128.5 2.6 copy.105
  131.1 1.8 convolution_bitcast_fusion.2
  135.7 30.5 %reduce-scatter.7.cloned.1.call-done = bf16[128,1024]{1,0:T(8,128)(2,1)} async-done(((bf16[1024,1024]{1,0:T(8,128)(2,1)}), bf16[128,1024]{1,0:T(8,128)(2,1)}) %reduce-scatter.7.cloned.1.call-update) | async-done | bytes 262160
  166.2 1.8 copy.124
  168.0 13.7 %collective-permute-done.3 = bf16[2,256,1024]{2,1,0:T(8,128)(2,1)} collective-permute-done((bf16[2,256,1024]{2,1,0:T(8,128)(2,1)}, bf16[2,256,1024]{2,1,0:T(8,128)(2,1)}, u32[]{:S(2)}, u32[]{:S(2)}) %collective-permute-start.3) | collective-permute-done | bytes 1048608 | tf_op jit(solution)/shard_map/ppermute | solution.py:15
  181.8 21.0 %collective-permute-done.2 = bf16[2,256,1024]{2,1,0:T(8,128)(2,1)} collective-permute-done((bf16[2,256,1024]{2,1,0:T(8,128)(2,1)}, bf16[2,256,1024]{2,1,0:T(8,128)(2,1)}, u32[]{:S(2)}, u32[]{:S(2)}) %collective-permute-start.2) | collective-permute-done | bytes 1048608 | tf_op jit(solution)/shard_map/ppermute | solution.py:15
  202.8 2.5 fusion.1
  206.4 48.9 %reduce-scatter.5.cloned.1.call-done = bf16[32,128]{1,0:T(8,128)(2,1)} async-done(((bf16[1024,128]{1,0:T(8,128)(2,1)}), bf16[32,128]{1,0:T(8,128)(2,1)}) %reduce-scatter.5.cloned.1.call-update) | async-done | bytes 8208 | tf_op jit(solution)/shard_map/reduce_scatter | solution.py:178
  (136 shorter events, 40.3 us)
Async XLA Ops:
  7.2 84.1 %copy-start = (bf16[1024,1024]{1,0:T(8,128)(2,1)S(1)}, bf16[1024,1024]{1,0:T(8,128)(2,1)}, u32[]{:S(2)}) copy-start(bf16[1024,1024]{1,0:T(8,128)(2,1)} %param.15) | copy-start | bytes 6291460
  7.2 11.0 %copy-start.34 = (s32[768]{0:T(1024)S(1)}, s32[768]{0:T(1024)}, u32[]{:S(2)}) copy-start(s32[768]{0:T(1024)} %param.17) | copy-start | bytes 9220
  7.2 11.0 %copy-start.33 = (f32[8,128]{1,0:T(8,128)S(1)}, f32[8,128]{1,0:T(8,128)}, u32[]{:S(2)}) copy-start(f32[8,128]{1,0:T(8,128)} %param.16) | copy-start | bytes 12292
  7.2 11.6 %copy-start.32 = (s32[1,8]{1,0:T(1,128)S(1)}, s32[1,8]{1,0:T(1,128)}, u32[]{:S(2)}) copy-start(s32[1,8]{1,0:T(1,128)} %param.18) | copy-start | bytes 100
  7.2 159.0 %reduce-scatter.7.cloned.1.call-start = ((), (), s32[]{:S(2)}) async-start(), calls=%async_computation.3 | async-start | bytes 2359296
  8.6 54.7 %copy-start.4 = (bf16[1,256,1024]{1,2,0:T(8,128)(2,1)}, bf16[1,256,1024]{1,2,0:T(8,128)(2,1)S(1)}, u32[]{:S(2)}) copy-start(bf16[1,256,1024]{1,2,0:T(8,128)(2,1)S(1)} %copy.126) | copy-start | bytes 1572868
  11.2 56.8 %collective-permute-start.1 = (bf16[2,256,1024]{1,2,0:T(8,128)(2,1)}, bf16[2,256,1024]{1,2,0:T(8,128)(2,1)}, u32[]{:S(2)}, u32[]{:S(2)}) collective-permute-start(bf16[2,256,1024]{1,2,0:T(8,128)(2,1)} %pad_maximum_fusion), channel_id=1, source_target_pairs={{6,0},{7,1},{0,2},{1,3},{2,4},{3,5},{4,6},{5,7},{14,8},{15,9},{8,1... | collective-permute-start | bytes 3145736 | tf_op jit(solution)/shard_map/ppermute | solution.py:15
  14.4 68.3 %collective-permute-start = (bf16[2,256,1024]{1,2,0:T(8,128)(2,1)}, bf16[2,256,1024]{1,2,0:T(8,128)(2,1)}, u32[]{:S(2)}, u32[]{:S(2)}) collective-permute-start(bf16[2,256,1024]{1,2,0:T(8,128)(2,1)} %pad_maximum_fusion), channel_id=1, source_target_pairs={{7,0},{0,1},{1,2},{2,3},{3,4},{4,5},{5,6},{6,7},{15,8},{8,9},{9,10... | collective-permute-start | bytes 3145736 | tf_op jit(solution)/shard_map/ppermute | solution.py:15
  26.8 57.3 %copy-start.2 = (bf16[1,256,1024]{1,2,0:T(8,128)(2,1)}, bf16[1,256,1024]{1,2,0:T(8,128)(2,1)S(1)}, u32[]{:S(2)}) copy-start(bf16[1,256,1024]{1,2,0:T(8,128)(2,1)S(1)} %copy.125) | copy-start | bytes 1572868
  63.4 4.1 %copy-start.19 = (bf16[32,8,8,128]{3,2,1,0:T(8,128)(2,1)S(1)}, bf16[32,8,8,128]{3,2,1,0:T(8,128)(2,1)}, u32[]{:S(2)}) copy-start(bf16[32,8,8,128]{3,2,1,0:T(8,128)(2,1)} %copy.128) | copy-start | bytes 1572868
  67.4 2.4 copy-start.13
  67.4 2.9 %copy-start.7 = (f32[8,256,511]{2,1,0:T(8,128)S(1)}, f32[8,256,511]{2,1,0:T(8,128)}, u32[]{:S(2)}) copy-start(f32[8,256,511]{2,1,0:T(8,128)} %reshape.304) | copy-start | bytes 12558340
  69.8 2.7 %copy-start.28 = (bf16[1,256,1024]{1,2,0:T(8,128)(2,1)}, bf16[1,256,1024]{1,2,0:T(8,128)(2,1)S(1)}, u32[]{:S(2)}) copy-start(bf16[1,256,1024]{1,2,0:T(8,128)(2,1)S(1)} %get-tuple-element.30) | copy-start | bytes 1572868
  69.8 16.9 %copy-start.30 = (bf16[1,256,1024]{1,2,0:T(8,128)(2,1)}, bf16[1,256,1024]{1,2,0:T(8,128)(2,1)S(1)}, u32[]{:S(2)}) copy-start(bf16[1,256,1024]{1,2,0:T(8,128)(2,1)S(1)} %get-tuple-element.31) | copy-start | bytes 1572868
  70.3 13.7 %copy-start.6 = (f32[8,256,511]{2,1,0:T(8,128)S(1)}, f32[8,256,511]{2,1,0:T(8,128)}, u32[]{:S(2)}) copy-start(f32[8,256,511]{2,1,0:T(8,128)} %reshape.302) | copy-start | bytes 12558340
  72.6 14.2 %copy-start.16 = (bf16[8,256,256]{2,1,0:T(8,128)(2,1)}, bf16[8,256,256]{2,1,0:T(8,128)(2,1)S(1)}, u32[]{:S(2)}) copy-start(bf16[8,256,256]{2,1,0:T(8,128)(2,1)S(1)} %get-tuple-element.50) | copy-start | bytes 3145732
  88.9 2.3 copy-start.12
  88.9 2.3 copy-start.18
  88.9 2.4 copy-start.31
  98.2 3.7 %copy-start.17 = (bf16[8,256,256]{2,1,0:T(8,128)(2,1)S(1)}, bf16[8,256,256]{2,1,0:T(8,128)(2,1)}, u32[]{:S(2)}) copy-start(bf16[8,256,256]{2,1,0:T(8,128)(2,1)} %copy-done.16) | copy-start | bytes 3145732
  98.2 157.1 %reduce-scatter.5.cloned.1.call-start = ((), (), s32[]{:S(2)}) async-start(), calls=%async_computation.2 | async-start | bytes 270336 | tf_op jit(solution)/shard_map/reduce_scatter | solution.py:178
  100.5 2.7 %copy-start.24 = (bf16[1,256,1024]{1,2,0:T(8,128)(2,1)S(1)}, bf16[1,256,1024]{1,2,0:T(8,128)(2,1)}, u32[]{:S(2)}) copy-start(bf16[1,256,1024]{1,2,0:T(8,128)(2,1)} %copy-done.23) | copy-start | bytes 1572868
  103.2 2.7 %copy-start.3 = (bf16[1,256,1024]{1,2,0:T(8,128)(2,1)S(1)}, bf16[1,256,1024]{1,2,0:T(8,128)(2,1)}, u32[]{:S(2)}) copy-start(bf16[1,256,1024]{1,2,0:T(8,128)(2,1)} %copy-done.2) | copy-start | bytes 1572868
  111.1 3.3 %copy-start.26 = (bf16[1,256,1024]{2,1,0:T(8,128)(2,1)S(1)}, bf16[1,256,1024]{2,1,0:T(8,128)(2,1)}, u32[]{:S(2)}) copy-start(bf16[1,256,1024]{2,1,0:T(8,128)(2,1)} %copy.114) | copy-start | bytes 1572868
  114.3 5.5 %copy-start.27 = (bf16[1,256,1024]{2,1,0:T(8,128)(2,1)S(1)}, bf16[1,256,1024]{2,1,0:T(8,128)(2,1)}, u32[]{:S(2)}) copy-start(bf16[1,256,1024]{2,1,0:T(8,128)(2,1)} %copy.109) | copy-start | bytes 1572868
  114.3 8.7 %copy-start.14 = (bf16[8,256,256]{2,1,0:T(8,128)(2,1)S(1)}, bf16[8,256,256]{2,1,0:T(8,128)(2,1)}, u32[]{:S(2)}) copy-start(bf16[8,256,256]{2,1,0:T(8,128)(2,1)} %copy-done.13) | copy-start | bytes 3145732
  116.6 7.8 %copy-start.20 = (bf16[32,8,8,128]{3,2,1,0:T(8,128)(2,1)S(1)}, bf16[32,8,8,128]{3,2,1,0:T(8,128)(2,1)}, u32[]{:S(2)}) copy-start(bf16[32,8,8,128]{3,2,1,0:T(8,128)(2,1)} %copy.128) | copy-start | bytes 1572868
  116.6 7.8 %copy-start.35 = (f32[8,256,256]{2,1,0:T(8,128)S(1)}, f32[8,256,256]{2,1,0:T(8,128)}, u32[]{:S(2)}) copy-start(f32[8,256,256]{2,1,0:T(8,128)} %get-tuple-element.47) | copy-start | bytes 6291460
  116.6 65.2 %collective-permute-start.3 = (bf16[2,256,1024]{2,1,0:T(8,128)(2,1)}, bf16[2,256,1024]{2,1,0:T(8,128)(2,1)}, u32[]{:S(2)}, u32[]{:S(2)}) collective-permute-start(bf16[2,256,1024]{2,1,0:T(8,128)(2,1)} %pad_maximum_fusion.2), channel_id=1, source_target_pairs={{2,0},{3,1},{4,2},{5,3},{6,4},{7,5},{0,6},{1,7},{10,8},{11,9},{12,... | collective-permute-start | bytes 3145736 | tf_op jit(solution)/shard_map/ppermute | solution.py:15
  120.9 81.8 %collective-permute-start.2 = (bf16[2,256,1024]{2,1,0:T(8,128)(2,1)}, bf16[2,256,1024]{2,1,0:T(8,128)(2,1)}, u32[]{:S(2)}, u32[]{:S(2)}) collective-permute-start(bf16[2,256,1024]{2,1,0:T(8,128)(2,1)} %pad_maximum_fusion.1), channel_id=1, source_target_pairs={{1,0},{2,1},{3,2},{4,3},{5,4},{6,5},{7,6},{0,7},{9,8},{10,9},{11,1... | collective-permute-start | bytes 3145736 | tf_op jit(solution)/shard_map/ppermute | solution.py:15
  126.9 4.2 %copy-start.5 = (bf16[1,256,1024]{1,2,0:T(8,128)(2,1)S(1)}, bf16[1,256,1024]{1,2,0:T(8,128)(2,1)}, u32[]{:S(2)}) copy-start(bf16[1,256,1024]{1,2,0:T(8,128)(2,1)} %copy-done.4) | copy-start | bytes 1572868
  202.8 53.8 %copy-start.1 = (bf16[1024,1024]{1,0:T(8,128)(2,1)S(1)}, bf16[1024,1024]{1,0:T(8,128)(2,1)}, u32[]{:S(2)}) copy-start(bf16[1024,1024]{1,0:T(8,128)(2,1)} %param.15) | copy-start | bytes 6291460
  (10 other events, 15.0 us)
Sparse Core Ops, SparseCore 0:
  98.3 67.8 reduce-scatter.6
  169.9 85.3 reduce-scatter.4
where the time goes:
time: 264 us; the launch traced here: 263 us
  waiting for transfers between devices  124 us (47%)
  local copies, waits for them, and re-layouts  66.2 us (25%)
  matrix products  28.1 us (11%)
  between operations  16.5 us (6%)
  other arithmetic  16.4 us (6%)
  starting transfers between devices  11.9 us (5%)
    reduce_scatter x1, waiting for transfers between devices, on_device(): lax.psum_scatter(shared_terms, 'dp', scatter_dimension=0, tiled=True)  48.9 us
    ppermute x4, waiting for transfers between devices, passed_along(): return lax.ppermute(block, axis, route)  44.9 us
    unnamed x3, waiting for transfers between devices  30.6 us
    reshape x3, local copies, waits for them, and re-layouts, toeplitz_bias(): tiled[:, :block_rows * (2 * block_rows - 1)]  23.8 us
    unnamed x83, local copies, waits for them, and re-layouts  13.3 us
    ppermute x4, starting transfers between devices, passed_along(): return lax.ppermute(block, axis, route)  11.8 us
    another operation x6, local copies, waits for them, and re-layouts, on_device(): jnp.stack([d_key.reshape(block_rows, model_width), d_value.reshape(block_...  9.61 us
    dot_general x3, matrix products, on_device(): jnp.einsum('rhe,che->hrc', query_heads, key_heads, preferred_element_type...  8.51 us
  transfers between devices with their start and end apart: 6, of which 5 were waited for; matrix products, arithmetic and copies ran while one was open for 33% of the time, Pallas kernels for 0%

commit v1 on v0

v1 whole, which is shorter than its diff:
```python
import functools

import jax
import jax.numpy as jnp
from jax import lax
from jax.experimental import pallas as pl
from jax.experimental.pallas import tpu as pltpu
from jax.sharding import PartitionSpec as P

MESH = pl.DeviceIdType.MESH
F32 = jnp.float32
BF16 = jnp.bfloat16
EPS = 1e-05
HEADS = 8
HD = 128
ROWS = 256
HALF = 128
NCH = 16
SCALE = HD ** (-0.5)
GRIDS = {32: (4, 4, 2), 8: (2, 2, 2), 4: (1, 2, 2), 2: (1, 1, 2), 1: (1, 1, 1)}

LF = 2
LG = 4
LH = 6
SD = LH + 8
SFD = SD + 2
SB = SFD + 2
SC = SB + 2
SE = SC + 2
AHEAD = 2


def dot_nn(a, b):
    return lax.dot_general(a, b, (((1,), (0,)), ((), ())), preferred_element_type=F32)


def dot_nt(a, b):
    return lax.dot_general(a, b, (((1,), (1,)), ((), ())), preferred_element_type=F32)


def dot_tn(a, b):
    return lax.dot_general(a, b, (((0,), (0,)), ((), ())), preferred_element_type=F32)


def kernel(
    grid,
    n_ctx,
    q_hbm,
    k_hbm,
    v_hbm,
    g_hbm,
    c_hbm,
    w_hbm,
    pb_ref,
    db_ref,
    hl_ref,
    fd_ref,
    dq_hbm,
    dk_hbm,
    dv_hbm,
    dg_hbm,
    dw_ref,
    q0,
    k0,
    v0,
    g0,
    c0,
    w0,
    idx,
    vtab,
    tb,
    qin,
    p1f,
    mx,
    pout,
    pin,
    asav,
    dsav,
    dgf,
    dnc,
    gt,
    dm0,
    dmin,
    r0f,
    r1f,
    rout,
    rin,
    dka,
    dva,
    oq,
    ok,
    ov,
    og,
    wbuf,
    cin,
    c1,
    ain,
    bin_,
    a2,
    b2,
    a3in,
    b3in,
    fbuf,
    fin,
    lsem,
    osem,
    qs,
    qr,
    ps,
    pr,
    ds_,
    dr,
    rs,
    rr,
    cs,
    cr,
    as_,
    ar,
    bs,
    br,
    a3s,
    a3r,
    b3s,
    b3r,
    fs,
    fr,
):
    nx, ny, nc = grid
    dp = lax.axis_index("dp")
    ctx = lax.axis_index("ctx")
    xi = lax.div(dp, ny * nc)
    yi = lax.rem(lax.div(dp, nc), ny)
    ci = lax.rem(dp, nc)
    left = (dp, lax.rem(ctx + n_ctx - 1, n_ctx))
    right = (dp, lax.rem(ctx + 1, n_ctx))

    def at_x(k):
        return lax.rem(xi + k, nx)

    def at_y(k):
        return lax.rem(yi + k, ny)

    def dev(x, y, c):
        return (x * (ny * nc) + y * nc + c, ctx)

    other = 1 - ci
    peers = [(dp, lax.rem(ctx + k, n_ctx)) for k in range(1, n_ctx)]
    peers += [dev(at_x(k), yi, ci) for k in range(1, nx)]
    peers += [dev(xi, at_y(k), ci) for k in range(1, ny)]
    if nc > 1:
        peers.append(dev(xi, yi, other))

    loads = [
        pltpu.make_async_copy(src.at[0] if lead else src, dst, lsem.at[i])
        for i, (src, dst, lead) in enumerate(
            (
                (q_hbm, q0, True),
                (k_hbm, k0, True),
                (v_hbm, v0, True),
                (c_hbm, c0, True),
                (w_hbm, w0, False),
                (g_hbm, g0, True),
            )
        )
    ]
    barrier = pltpu.get_barrier_semaphore()
    for peer in peers:
        pl.semaphore_signal(barrier, inc=1, device_id=peer, device_id_type=MESH)
    for load in loads:
        load.start()

    block = lax.rem(ctx - fd_ref[0] + n_ctx, n_ctx)
    end = jnp.int32(0)
    inner = jnp.int32(0)
    user_len = jnp.int32(0)
    user_blocks = jnp.int32(0)
    for i in range(8):
        length = hl_ref[0, i]
        count = lax.div(length + (ROWS - 1), ROWS)
        start = end
        end = end + count
        inside = (start <= block) & (block < end)
        inner = jnp.where(inside, block - start, inner)
        user_len = jnp.where(inside, length, user_len)
        user_blocks = jnp.where(inside, count, user_blocks)
    live_rows = user_len - inner * ROWS
    valid = [
        None,
        (inner + 1 < user_blocks).astype(jnp.int32).astype(F32),
        (inner + 2 < user_blocks).astype(jnp.int32).astype(F32),
    ]

    def remote(src, dst, ssem, rsem, device):
        return pltpu.make_async_remote_copy(
            src_ref=src,
            dst_ref=dst,
            send_sem=ssem,
            recv_sem=rsem,
            device_id=device,
            device_id_type=MESH,
        )

    def half_of(n):
        return n // HEADS if isinstance(n, int) else lax.div(n, HEADS)

    def head_of(n):
        return n % HEADS if isinstance(n, int) else lax.rem(n, HEADS)

    def rows_of(n):
        r = half_of(n)
        return pl.ds(r * HALF if isinstance(n, int) else pl.multiple_of(r * HALF, HALF), HALF)

    def cols_of(n):
        h = head_of(n)
        return pl.ds(h * HD if isinstance(n, int) else pl.multiple_of(h * HD, HD), HD)

    def q_own(n):
        return remote(q0.at[rows_of(n), cols_of(n)], qin.at[0, n], qs.at[0, n], qr.at[0, n], left)

    def q_fwd(n):
        return remote(qin.at[0, n], qin.at[1, n], qs.at[1, n], qr.at[1, n], left)

    def p_two(n):
        return remote(pout.at[1, n], pin.at[1, n], ps.at[1, n], pr.at[1, n], right)

    def p_one(n):
        return remote(pout.at[0, n], pin.at[0, n], ps.at[0, n], pr.at[0, n], right)

    def d_own(n):
        return remote(dm0.at[n], dmin.at[0, n], ds_.at[0, n], dr.at[0, n], left)

    def d_fwd(n):
        return remote(dmin.at[0, n], dmin.at[1, n], ds_.at[1, n], dr.at[1, n], left)

    def r_two(n):
        return remote(rout.at[1, n], rin.at[1, n], rs.at[1, n], rr.at[1, n], right)

    def r_one(n):
        return remote(rout.at[0, n], rin.at[0, n], rs.at[0, n], rr.at[0, n], right)

    def tables():
        for m in range(6):
            idx[m : m + 1, :] = db_ref[m * HD : (m + 1) * HD].astype(F32).reshape(1, HD)
        idx[6:8, :] = jnp.zeros((2, HD), F32)
        rowi = lax.broadcasted_iota(jnp.int32, (HD, HD), 0)
        coli = lax.broadcasted_iota(jnp.int32, (HD, HD), 1)
        turn = jnp.where(rowi + coli == HD, 1.0, 0.0) + jnp.where(
            (rowi == 0) & (coli == 0), 1.0, 0.0
        )
        turned = dot_nn(idx[...].astype(BF16), turn.astype(BF16))
        lane = lax.broadcasted_iota(jnp.int32, (1, HD), 1)
        bias = pb_ref[...] * 0.5
        hi = bias.astype(BF16)
        rest = bias - hi.astype(F32)
        mid = rest.astype(BF16)
        low = (rest - mid.astype(F32)).astype(BF16)
        for m in range(7):
            before = turned[max(m - 1, 0) : max(m - 1, 0) + 1, :]
            here = turned[m : m + 1, :]
            want = jnp.where(lane == 0, here, before)
            hot = jnp.where(
                rowi.astype(F32) == jnp.broadcast_to(want, (HD, HD)), 1.0, 0.0
            ).astype(BF16)
            vtab[:, m * HD : (m + 1) * HD] = (
                dot_nn(hi, hot) + dot_nn(mid, hot) + dot_nn(low, hot)
            )

        def one_head(h, carry):
            tb[h, 0] = jnp.zeros((HD, HD), F32)
            for m in range(6):
                line = vtab[pl.ds(h, 1), m * HD : (m + 2) * HD]
                wide = jnp.broadcast_to(line, (HD, 2 * HD))
                tb[h, m + 1] = pltpu.roll(wide, 0, 1, stride=1, stride_axis=0)[:, :HD]
            return carry

        lax.fori_loop(0, HEADS, one_head, 0)

    def forward(n):
        r, h = half_of(n), head_of(n)
        kh, vh = k0[:, cols_of(n)], v0[:, cols_of(n)]
        for o in (2, 1, 0):
            qc = q0[rows_of(n), cols_of(n)] if o == 0 else qin[o - 1, n]
            bias = jnp.concatenate([tb[h, 2 * o + r + 1], tb[h, 2 * o + r]], axis=1)
            x = dot_nt(qc, kh) * (0.5 * SCALE) + bias
            th = jnp.tanh(x)
            u = 1.0 + th
            a = x * u
            d = u + a * (1.0 - th)
            if o == 0:
                row = lax.broadcasted_iota(jnp.int32, (HALF, ROWS), 0) + r * HALF
                col = lax.broadcasted_iota(jnp.int32, (HALF, ROWS), 1)
                a = jnp.where(col <= row, a, 0.0)
                d = jnp.where(col <= row, d, 0.0)
            a = a.astype(BF16)
            asav[o, n] = a
            dsav[o, n] = d
            part = dot_nn(a, vh)
            if o == 2:
                pout[1, n] = (part * valid[2]).astype(BF16)
                p_two(n).start()
            elif o == 1:
                p1f[n] = part * valid[1]
            else:
                mx[n] = part

    def backward(n):
        h = head_of(n)
        kh, vh = k0[:, cols_of(n)], v0[:, cols_of(n)]
        dss, dms = [], []
        for o in (2, 1, 0):
            if o == 0:
                dmc = dm0[n]
            else:
                dmc = (dmin[o - 1, n].astype(F32) * valid[o]).astype(BF16)
            dsc = (dot_nt(dmc, vh) * dsav[o, n]).astype(BF16)
            part = dot_nn(dsc, kh)
            if o == 2:
                rout[1, n] = part.astype(BF16)
                r_two(n).start()
            elif o == 1:
                r1f[n] = part
            else:
                r0f[n] = part
            dss.append(dsc)
            dms.append(dmc)
        qs3 = jnp.concatenate([qin[1, n], qin[0, n], q0[rows_of(n), cols_of(n)]], axis=0)
        dka[h] += dot_tn(jnp.concatenate(dss, axis=0), qs3)
        as3 = jnp.concatenate([asav[2, n], asav[1, n], asav[0, n]], axis=0)
        dva[h] += dot_tn(as3, jnp.concatenate(dms, axis=0))

    def live_mask(r, width):
        row = lax.broadcasted_iota(jnp.int32, (HALF, width), 0) + r * HALF
        return row < live_rows

    def gate_of(r, h):
        return g0[r * HALF : (r + 1) * HALF, h * HD : (h + 1) * HD].astype(F32)

    def d_gated():
        for i in (3, 4, 5):
            loads[i].wait()
        for pair in range(4):
            got = dot_nt(c0[...], w0[pair * 256 : (pair + 1) * 256, :])
            for r in range(2):
                for j in range(2):
                    h = 2 * pair + j
                    dgf[r * HEADS + h] = got[
                        r * HALF : (r + 1) * HALF, j * HD : (j + 1) * HD
                    ]
        for r in range(2):
            mask = live_mask(r, HD)
            total = jnp.zeros((HALF, HD), F32)
            for h in range(HEADS):
                dn = jnp.where(mask, dgf[r * HEADS + h] * gate_of(r, h), 0.0)
                dnc[r * HEADS + h] = dn
                total = total + dn
            mean = jnp.sum(total, axis=1, keepdims=True) * (1.0 / (HEADS * HD))
            for h in range(HEADS):
                dnc[r * HEADS + h] = dnc[r * HEADS + h] - mean

    def norm(r):
        inv_n = 1.0 / (HEADS * HD)
        total = mx[r * HEADS]
        for h in range(1, HEADS):
            total = total + mx[r * HEADS + h]
        mean = jnp.sum(total, axis=1, keepdims=True) * inv_n
        square = jnp.zeros((HALF, HD), F32)
        cross = jnp.zeros((HALF, HD), F32)
        for h in range(HEADS):
            cen = mx[r * HEADS + h] - mean
            mx[r * HEADS + h] = cen
            square = square + cen * cen
            cross = cross + cen * dnc[r * HEADS + h]
        inv = lax.rsqrt(jnp.sum(square, axis=1, keepdims=True) * inv_n + EPS)
        slope = jnp.sum(cross, axis=1, keepdims=True) * inv_n * inv * inv
        for h in range(HEADS):
            n = r * HEADS + h
            dm0[n] = (inv * (dnc[n] - mx[n] * slope)).astype(BF16)

        mask = live_mask(r, HD)
        rows = slice(r * HALF, (r + 1) * HALF)
        for h in range(HEADS):
            n = r * HEADS + h
            cols = slice(h * HD, (h + 1) * HD)
            normed = mx[n] * inv
            gt[rows, cols] = jnp.where(mask, normed * gate_of(r, h), 0.0).astype(BF16)
            og[rows, cols] = jnp.where(mask, dgf[n] * normed, 0.0).astype(BF16)

    rw = 1024 // (nx * ny * nc)

    def core_copy(x):
        return remote(wbuf.at[other, x], cin.at[x], cs.at[x], cr.at[x], dev(xi, yi, other))

    def a_copy(k):
        return remote(
            c1.at[at_x(k), :, 0], ain.at[k - 1], as_.at[k - 1], ar.at[k - 1], dev(at_x(k), yi, ci)
        )

    def b_copy(k):
        return remote(
            c1.at[:, at_y(k), 1], bin_.at[k - 1], bs.at[k - 1], br.at[k - 1], dev(xi, at_y(k), ci)
        )

    def a3_copy(k):
        return remote(
            a2.at[at_y(k)], a3in.at[k - 1], a3s.at[k - 1], a3r.at[k - 1], dev(xi, at_y(k), ci)
        )

    def b3_copy(k):
        return remote(
            b2.at[at_x(k)], b3in.at[k - 1], b3s.at[k - 1], b3r.at[k - 1], dev(at_x(k), yi, ci)
        )

    def f_copy(k):
        to = lax.rem(ctx + k, n_ctx)
        return remote(fbuf.at[to], fin.at[k - 1], fs.at[k - 1], fr.at[k - 1], (dp, to))

    def weight_terms():
        rx = 1024 // nx
        for x in range(nx):
            for half in range(2):
                got = dot_tn(
                    gt[:, x * rx : (x + 1) * rx], c0[:, half * 512 : (half + 1) * 512]
                ).astype(BF16)
                for y in range(ny):
                    for c in range(nc):
                        at = (y * nc + c) * rw
                        wbuf[c, x, y, half] = got[at : at + rw, :]
            if nc > 1:
                core_copy(x).start()

    def after_core():
        for x in range(nx):
            if nc > 1:
                core_copy(x).wait_recv()
            for y in range(ny):
                for half in range(2):
                    got = wbuf[ci, x, y, half].astype(F32)
                    if nc > 1:
                        got = got + cin[x, y, half].astype(F32)
                    c1[x, y, half] = got.astype(BF16)
        for k in range(1, nx):
            a_copy(k).start()
        for k in range(1, ny):
            b_copy(k).start()

    def after_two():
        for k in range(1, nx):
            a_copy(k).wait_recv()
        for y in range(ny):
            got = c1[xi, y, 0].astype(F32)
            for k in range(1, nx):
                got = got + ain[k - 1, y].astype(F32)
            a2[y] = got.astype(BF16)
        for k in range(1, ny):
            a3_copy(k).start()
        for k in range(1, ny):
            b_copy(k).wait_recv()
        for x in range(nx):
            got = c1[x, yi, 1].astype(F32)
            for k in range(1, ny):
                got = got + bin_[k - 1, x].astype(F32)
            b2[x] = got.astype(BF16)
        for k in range(1, nx):
            b3_copy(k).start()

    def after_three():
        for k in range(1, ny):
            a3_copy(k).wait_recv()
        got = a2[yi].astype(F32)
        for k in range(1, ny):
            got = got + a3in[k - 1].astype(F32)
        for c in range(4):
            fbuf[c] = got[:, c * HD : (c + 1) * HD].astype(BF16)
        for k in range(1, nx):
            b3_copy(k).wait_recv()
        got = b2[xi].astype(F32)
        for k in range(1, nx):
            got = got + b3in[k - 1].astype(F32)
        for c in range(4):
            fbuf[4 + c] = got[:, c * HD : (c + 1) * HD].astype(BF16)
        for k in range(1, n_ctx):
            f_copy(k).start()

    def after_four():
        for k in range(1, n_ctx):
            f_copy(k).wait_recv()
        got = fbuf[ctx].astype(F32)
        for k in range(1, n_ctx):
            got = got + fin[k - 1].astype(F32)
        dw_ref[...] = got

    outs = [
        pltpu.make_async_copy(src, dst.at[0], osem.at[i])
        for i, (src, dst) in enumerate(
            ((oq, dq_hbm), (ok, dk_hbm), (ov, dv_hbm), (og, dg_hbm))
        )
    ]

    def keys_out():
        for h in range(HEADS):
            cols = slice(h * HD, (h + 1) * HD)
            ok[:, cols] = (dka[h] * (0.5 * SCALE)).astype(BF16)
            ov[:, cols] = dva[h].astype(BF16)
        outs[1].start()
        outs[2].start()

    def st_q_own(n):
        q_own(n).start()

    def st_q_fwd(n):
        q_own(n).wait_recv()
        q_fwd(n).start()

    def st_forward(n):
        q_fwd(n).wait_recv()
        forward(n)

    def st_g(n):
        p_two(n).wait_recv()
        pout[0, n] = (p1f[n] + pin[1, n].astype(F32)).astype(BF16)
        p_one(n).start()

    def st_h(n):
        p_one(n).wait_recv()
        mx[n] += pin[0, n].astype(F32)

    def st_d_own(n):
        d_own(n).start()

    def st_d_fwd(n):
        d_own(n).wait_recv()
        d_fwd(n).start()

    def st_backward(n):
        d_fwd(n).wait_recv()
        backward(n)

    def st_c(n):
        r_two(n).wait_recv()
        rout[0, n] = (r1f[n] + rin[1, n].astype(F32)).astype(BF16)
        r_one(n).start()

    def st_e(n):
        r_one(n).wait_recv()
        oq[rows_of(n), cols_of(n)] = (
            (r0f[n] + rin[0, n].astype(F32)) * (0.5 * SCALE)
        ).astype(BF16)

    stages = (
        (st_q_own, -AHEAD),
        (st_d_own, SD),
        (st_q_fwd, 0),
        (st_d_fwd, SFD),
        (st_g, LG),
        (st_c, SC),
        (st_forward, LF),
        (st_backward, SB),
        (st_h, LH),
        (st_e, SE),
    )
    after = {
        5: [d_gated],
        LH + 7: [functools.partial(norm, 0)],
        LH + 15: [functools.partial(norm, 1), weight_terms, outs[3].start],
        LH + 18: [after_core],
        LH + 23: [after_two],
        LH + 27: [after_three, keys_out],
        SE + 15: [after_four],
    }

    loads[0].wait()
    pl.semaphore_wait(barrier, len(peers))
    for n in range(AHEAD):
        q_own(n).start()
    tables()
    loads[1].wait()
    loads[2].wait()
    dka[...] = jnp.zeros_like(dka)
    dva[...] = jnp.zeros_like(dva)

    last = SE + NCH

    def active(s):
        return tuple(0 <= s - at < NCH for _, at in stages)

    s = 0
    while s < last:
        e = s + 1
        while e < last and active(e) == active(s) and (e - 1) not in after:
            e += 1
        todo = [stage for stage, on in zip(stages, active(s)) if on]

        def slot(i, carry, todo=todo):
            for fn, at in todo:
                fn(i - at)
            return carry

        if e - s == 1:
            slot(s, 0)
        else:
            lax.fori_loop(s, e, slot, 0)
        for fn in after.get(e - 1, ()):
            fn()
        s = e
    outs[0].start()

    def drain(n, carry):
        for copy in (q_own, q_fwd, p_two, p_one, d_own, d_fwd, r_two, r_one):
            copy(n).wait_send()
        return carry

    lax.fori_loop(0, NCH, drain, 0)
    if nc > 1:
        for x in range(nx):
            core_copy(x).wait_send()
    for k in range(1, nx):
        a_copy(k).wait_send()
        b3_copy(k).wait_send()
    for k in range(1, ny):
        b_copy(k).wait_send()
        a3_copy(k).wait_send()
    for k in range(1, n_ctx):
        f_copy(k).wait_send()
    for out in outs:
        out.wait()


def on_device(q, k, v, g, c, w, pb, db, hl, fd):
    n_dp = lax.axis_size("dp")
    n_ctx = lax.axis_size("ctx")
    nx, ny, nc = grid = GRIDS[n_dp]
    rw = 1024 // n_dp
    chunk = (NCH, HALF, HD)
    vm = pltpu.VMEM
    dma = pltpu.SemaphoreType.DMA
    big = jax.ShapeDtypeStruct((1, ROWS, HEADS * HD), BF16)
    anyspec = pl.BlockSpec(memory_space=pl.ANY)
    vmem = pl.BlockSpec(memory_space=pltpu.VMEM)
    smem = pl.BlockSpec(memory_space=pltpu.SMEM)
    wide = vm((ROWS, HEADS * HD), BF16)
    return pl.pallas_call(
        functools.partial(kernel, grid, n_ctx),
        out_shape=(big, big, big, big, jax.ShapeDtypeStruct((rw, HD), F32)),
        in_specs=[anyspec] * 6 + [vmem, vmem, smem, smem],
        out_specs=[anyspec] * 4 + [vmem],
        scratch_shapes=[
            wide,
            wide,
            wide,
            wide,
            wide,
            vm((1024, 1024), BF16),
            vm((8, HD), F32),
            vm((HEADS, 7 * HD), F32),
            vm((HEADS, 7, HD, HD), F32),
            vm((2,) + chunk, BF16),
            vm(chunk, F32),
            vm(chunk, F32),
            vm((2,) + chunk, BF16),
            vm((2,) + chunk, BF16),
            vm((3, NCH, HALF, ROWS), BF16),
            vm((3, NCH, HALF, ROWS), F32),
            vm(chunk, F32),
            vm(chunk, F32),
            wide,
            vm(chunk, BF16),
            vm((2,) + chunk, BF16),
            vm(chunk, F32),
            vm(chunk, F32),
            vm((2,) + chunk, BF16),
            vm((2,) + chunk, BF16),
            vm((HEADS, ROWS, HD), F32),
            vm((HEADS, ROWS, HD), F32),
            wide,
            wide,
            wide,
            wide,
            vm((nc, nx, ny, 2, rw, 512), BF16),
            vm((nx, ny, 2, rw, 512), BF16),
            vm((nx, ny, 2, rw, 512), BF16),
            vm((max(nx - 1, 1), ny, rw, 512), BF16),
            vm((max(ny - 1, 1), nx, rw, 512), BF16),
            vm((ny, rw, 512), BF16),
            vm((nx, rw, 512), BF16),
            vm((max(ny - 1, 1), rw, 512), BF16),
            vm((max(nx - 1, 1), rw, 512), BF16),
            vm((8, rw, HD), BF16),
            vm((7, rw, HD), BF16),
            dma((6,)),
            dma((4,)),
        ]
        + [dma((2, NCH))] * 8
        + [dma((4,))] * 10
        + [dma((8,))] * 2,
        compiler_params=pltpu.CompilerParams(
            collective_id=0, has_side_effects=True, vmem_limit_bytes=60 * 1024 * 1024
        ),
    )(q, k, v, g, c, w, pb, db, hl, fd)


def solution(mesh):
    rows = P("dp", "ctx", None)
    return jax.shard_map(
        on_device,
        mesh=mesh,
        in_specs=(rows,) * 5 + (P(), P(), P(), P("dp", None), P("dp")),
        out_specs=(rows,) * 4 + (P("dp", "ctx"),),
        check_vma=False,
    )
```

time: 264 us -> 92.8 us (0.35)
  waiting for transfers between devices: 124 us -> 0 us
  Pallas kernels: 0 us -> 84.3 us
  local copies, waits for them, and re-layouts: 66.2 us -> 6.02 us
  matrix products: 28.1 us -> 0 us
  other arithmetic: 16.4 us -> 0 us
  between operations: 16.5 us -> 1.32 us
  starting transfers between devices: 11.9 us -> 0 us
    pallas_call x0 -> x1, Pallas kernels: none -> 84.3 us  [on_device(): pl.pallas_call(functools.partial(kernel, grid, n_ctx), out_shape=(big, bi...]
    reduce_scatter x1 -> x0, waiting for transfers between devices: 48.9 us -> none  [on_device(): lax.psum_scatter(shared_terms, 'dp', scatter_dimension=0, tiled=True)]
    ppermute x4 -> x0, waiting for transfers between devices: 44.9 us -> none  [passed_along(): return lax.ppermute(block, axis, route)]
    unnamed x3 -> x0, waiting for transfers between devices: 30.6 us -> none
    dot_general x21 -> x0, matrix products: 28.1 us -> none  [the longest x3 8.51 us: on_device(): jnp.einsum('rhe,che->hrc', query_heads, key_heads, preferred_element_type...]
    reshape x4 -> x0, local copies, waits for them, and re-layouts: 24 us -> none  [the longest x3 23.8 us: toeplitz_bias(): tiled[:, :block_rows * (2 * block_rows - 1)]]
    another operation x8 -> x0, local copies, waits for them, and re-layouts: 12.2 us -> none  [the longest x6 9.61 us: on_device(): jnp.stack([d_key.reshape(block_rows, model_width), d_value.reshape(block_...]
    ppermute x4 -> x0, starting transfers between devices: 11.8 us -> none  [passed_along(): return lax.ppermute(block, axis, route)]
  transfers between devices with their start and end apart: 6 -> 0, of which waited for: 5 -> 0; matrix products, arithmetic and copies ran while one was open for 33% -> 0% of each run, Pallas kernels for 0% -> 0%
where the time goes in v1:
time: 92.8 us; the launch traced here: 91.7 us
  Pallas kernels  84.3 us (91%)
  local copies, waits for them, and re-layouts  6.02 us (6%)
  between operations  1.32 us (1%)
    pallas_call x1, Pallas kernels, on_device(): pl.pallas_call(functools.partial(kernel, grid, n_ctx), out_shape=(big, bi...  84.3 us
    unnamed x11, local copies, waits for them, and re-layouts  6.02 us

profile of v1, /device:TPU:32, one launch (start us, length us, event | category | flops | bytes accessed | tf_op | source)
XLA Modules:
  0.0 91.7 jit_solution(4727185056467568530)
XLA Ops:
  1.3 84.3 %shard_map.137 = (bf16[1,256,1024]{2,1,0:T(8,128)(2,1)}, bf16[1,256,1024]{2,1,0:T(8,128)(2,1)}, bf16[1,256,1024]{2,1,0:T(8,128)(2,1)}, bf16[1,256,1024]{2,1,0:T(8,128)(2,1)}, f32[32,128]{1,0:T(8,128)}) custom-call(bf16[1,256,1024]{2,1,0:T(8,128)(2,1)} %q_hbm.1, bf16[1,256,1024]{2,1,0:T(8,128)(2,1)} %k_hbm.1, bf16[1,256,1024]{2,1,0:T(8,128)(2,1)} %v_hbm.1, ...), custom_call_target="tpu_custom_call" | custom-call | tf_op jit(solution)/shard_map/pallas_call | solution.py:641
  85.6 0.0 copy-start.1
  85.6 0.0 copy-start
  85.6 0.0 copy-start.2
  85.6 2.0 %copy.21 = bf16[1,256,1024]{2,1,0:T(8,128)(2,1)} copy(bf16[1,256,1024]{2,1,0:T(8,128)(2,1)} %get-tuple-element.10) | data formatting | bytes 1048576
  87.6 1.9 %copy.22 = bf16[1,256,1024]{2,1,0:T(8,128)(2,1)} copy(bf16[1,256,1024]{2,1,0:T(8,128)(2,1)} %get-tuple-element.11) | data formatting | bytes 1048576
  89.5 0.0 copy-done.1
  89.5 0.8 copy.23
  90.3 0.0 copy-done
  90.3 0.8 copy.24
  91.1 0.0 copy-done.2
  91.1 0.6 copy.25
Async XLA Ops:
  85.6 3.9 %copy-start.1 = (bf16[1,256,1024]{2,1,0:T(8,128)(2,1)S(1)}, bf16[1,256,1024]{2,1,0:T(8,128)(2,1)}, u32[]{:S(2)}) copy-start(bf16[1,256,1024]{2,1,0:T(8,128)(2,1)} %get-tuple-element.12) | copy-start | bytes 1572868
  85.6 4.6 %copy-start = (bf16[1,256,1024]{2,1,0:T(8,128)(2,1)S(1)}, bf16[1,256,1024]{2,1,0:T(8,128)(2,1)}, u32[]{:S(2)}) copy-start(bf16[1,256,1024]{2,1,0:T(8,128)(2,1)} %get-tuple-element.13) | copy-start | bytes 1572868
  85.6 5.4 %copy-start.2 = (f32[32,128]{1,0:T(8,128)S(1)}, f32[32,128]{1,0:T(8,128)}, u32[]{:S(2)}) copy-start(f32[32,128]{1,0:T(8,128)} %get-tuple-element.14) | copy-start | bytes 49156

commit v2 on v1

--- a/solution.py
+++ b/solution.py
@@ -1,4 +1,5 @@
 import functools
+import math
 
 import jax
 import jax.numpy as jnp
@@ -19,15 +20,21 @@
 SCALE = HD ** (-0.5)
 GRIDS = {32: (4, 4, 2), 8: (2, 2, 2), 4: (1, 2, 2), 2: (1, 1, 2), 1: (1, 1, 1)}
 
-LF = 2
-LG = 4
-LH = 6
-SD = LH + 8
-SFD = SD + 2
-SB = SFD + 2
-SC = SB + 2
-SE = SC + 2
-AHEAD = 2
+MID = 6
+PER = 7
+
+AHEAD = 4.0
+HOP = 3.5
+MIDLAG = 0.4
+T_OWN = 0.2
+T_GATED = 8.95
+D_LAG = 1.0
+T_CORE = 3.0
+T_TWO = 8.0
+T_THREE = 11.5
+T_FOUR = 14.5
+T_MID = 0.4
+DM = 2 * PER
 
 
 def dot_nn(a, b):
@@ -87,6 +94,12 @@
     rin,
     dka,
     dva,
+    kl,
+    vl,
+    dkl,
+    dvl,
+    sout,
+    sin,
     oq,
     ok,
     ov,
@@ -112,6 +125,10 @@
     dr,
     rs,
     rr,
+    ks,
+    kr,
+    ss,
+    sr,
     cs,
     cr,
     as_,
@@ -189,6 +206,7 @@
         (inner + 1 < user_blocks).astype(jnp.int32).astype(F32),
         (inner + 2 < user_blocks).astype(jnp.int32).astype(F32),
     ]
+    valid_mid = ((inner >= 1) & (inner + 1 < user_blocks)).astype(jnp.int32).astype(F32)
 
     def remote(src, dst, ssem, rsem, device):
         return pltpu.make_async_remote_copy(
@@ -237,6 +255,16 @@
 
     def r_one(n):
         return remote(rout.at[0, n], rin.at[0, n], rs.at[0, n], rr.at[0, n], right)
+
+    def kv_own(i):
+        src, dst = ((k0, kl), (v0, vl))[i % 2]
+        h = i // 2
+        return remote(
+            src.at[:, pl.ds((MID + h) * HD, HD)], dst.at[h], ks.at[i], kr.at[i], right
+        )
+
+    def kv_back(i):
+        return remote(sout.at[i], sin.at[i], ss.at[i], sr.at[i], left)
 
     def tables():
         for m in range(6):
@@ -275,43 +303,63 @@
 
         lax.fori_loop(0, HEADS, one_head, 0)
 
+    def curve(qc, kh, h, r, o):
+        bias = jnp.concatenate([tb[h, 2 * o + r + 1], tb[h, 2 * o + r]], axis=1)
+        x = dot_nt(qc, kh) * (0.5 * SCALE) + bias
+        th = jnp.tanh(x)
+        u = 1.0 + th
+        a = x * u
+        return a, u + a * (1.0 - th)
+
+    def forward_own(n):
+        r, h = half_of(n), head_of(n)
+        a, d = curve(q0[rows_of(n), cols_of(n)], k0[:, cols_of(n)], h, r, 0)
+        row = lax.broadcasted_iota(jnp.int32, (HALF, ROWS), 0) + r * HALF
+        col = lax.broadcasted_iota(jnp.int32, (HALF, ROWS), 1)
+        a = jnp.where(col <= row, a, 0.0).astype(BF16)
+        asav[0, n] = a
+        dsav[0, n] = jnp.where(col <= row, d, 0.0)
+        mx[n] = dot_nn(a, v0[:, cols_of(n)])
+
     def forward(n):
         r, h = half_of(n), head_of(n)
         kh, vh = k0[:, cols_of(n)], v0[:, cols_of(n)]
-        for o in (2, 1, 0):
-            qc = q0[rows_of(n), cols_of(n)] if o == 0 else qin[o - 1, n]
-            bias = jnp.concatenate([tb[h, 2 * o + r + 1], tb[h, 2 * o + r]], axis=1)
-            x = dot_nt(qc, kh) * (0.5 * SCALE) + bias
-            th = jnp.tanh(x)
-            u = 1.0 + th
-            a = x * u
-            d = u + a * (1.0 - th)
-            if o == 0:
-                row = lax.broadcasted_iota(jnp.int32, (HALF, ROWS), 0) + r * HALF
-                col = lax.broadcasted_iota(jnp.int32, (HALF, ROWS), 1)
-                a = jnp.where(col <= row, a, 0.0)
-                d = jnp.where(col <= row, d, 0.0)
+        for o in (2, 1):
+            a, d = curve(qin[o - 1, n], kh, h, r, o)
             a = a.astype(BF16)
             asav[o, n] = a
             dsav[o, n] = d
-            part = dot_nn(a, vh)
+            part = dot_nn(a, vh) * valid[o]
             if o == 2:
-                pout[1, n] = (part * valid[2]).astype(BF16)
+                pout[1, n] = part.astype(BF16)
                 p_two(n).start()
-            elif o == 1:
-                p1f[n] = part * valid[1]
             else:
-                mx[n] = part
+                p1f[n] = part
+
+    def forward_mid(n):
+        r, h = half_of(n), head_of(n)
+        total = None
+        for o in (1, 2):
+            kh = k0[:, cols_of(n)] if o == 1 else kl[h - MID]
+            vh = v0[:, cols_of(n)] if o == 1 else vl[h - MID]
+            a, d = curve(qin[0, n], kh, h, r, o)
+            a = a.astype(BF16)
+            asav[o, n] = a
+            dsav[o, n] = d
+            part = dot_nn(a, vh) * (valid[1] if o == 1 else valid_mid)
+            total = part if total is None else total + part
+        pout[0, n] = total.astype(BF16)
+        p_one(n).start()
+
+    def masked(x, flag):
+        return (x.astype(F32) * flag).astype(BF16)
 
     def backward(n):
         h = head_of(n)
         kh, vh = k0[:, cols_of(n)], v0[:, cols_of(n)]
         dss, dms = [], []
         for o in (2, 1, 0):
-            if o == 0:
-                dmc = dm0[n]
-            else:
-                dmc = (dmin[o - 1, n].astype(F32) * valid[o]).astype(BF16)
+            dmc = dm0[n] if o == 0 else masked(dmin[o - 1, n], valid[o])
             dsc = (dot_nt(dmc, vh) * dsav[o, n]).astype(BF16)
             part = dot_nn(dsc, kh)
             if o == 2:
@@ -327,6 +375,36 @@
         dka[h] += dot_tn(jnp.concatenate(dss, axis=0), qs3)
         as3 = jnp.concatenate([asav[2, n], asav[1, n], asav[0, n]], axis=0)
         dva[h] += dot_tn(as3, jnp.concatenate(dms, axis=0))
+
+    def backward_mid(n):
+        h = head_of(n)
+        i = h - MID
+        kh, vh = k0[:, cols_of(n)], v0[:, cols_of(n)]
+        near, far = masked(dmin[0, n], valid[1]), masked(dmin[0, n], valid_mid)
+        ds_far = (dot_nt(far, vl[i]) * dsav[2, n]).astype(BF16)
+        ds_near = (dot_nt(near, vh) * dsav[1, n]).astype(BF16)
+        rout[0, n] = (dot_nn(ds_near, kh) + dot_nn(ds_far, kl[i])).astype(BF16)
+        r_one(n).start()
+        ds_own = (dot_nt(dm0[n], vh) * dsav[0, n]).astype(BF16)
+        r0f[n] = dot_nn(ds_own, kh)
+        qn = qin[0, n]
+        dka[h] += dot_tn(
+            jnp.concatenate([ds_near, ds_own], axis=0),
+            jnp.concatenate([qn, q0[rows_of(n), cols_of(n)]], axis=0),
+        )
+        dva[h] += dot_tn(
+            jnp.concatenate([asav[1, n], asav[0, n]], axis=0),
+            jnp.concatenate([near, dm0[n]], axis=0),
+        )
+        dkl[i] += dot_tn(ds_far, qn)
+        dvl[i] += dot_tn(asav[2, n], far)
+
+    def mid_out():
+        for i in range(HEADS - MID):
+            sout[2 * i] = (dkl[i] * (0.5 * SCALE)).astype(BF16)
+            sout[2 * i + 1] = dvl[i].astype(BF16)
+            kv_back(2 * i).start()
+            kv_back(2 * i + 1).start()
 
     def live_mask(r, width):
         row = lax.broadcasted_iota(jnp.int32, (HALF, width), 0) + r * HALF
@@ -497,10 +575,19 @@
     ]
 
     def keys_out():
-        for h in range(HEADS):
+        for h in range(MID):
             cols = slice(h * HD, (h + 1) * HD)
             ok[:, cols] = (dka[h] * (0.5 * SCALE)).astype(BF16)
             ov[:, cols] = dva[h].astype(BF16)
+
+    def mid_in():
+        for h in range(MID, HEADS):
+            cols = slice(h * HD, (h + 1) * HD)
+            i = 2 * (h - MID)
+            kv_back(i).wait_recv()
+            ok[:, cols] = (dka[h] * (0.5 * SCALE) + sin[i].astype(F32)).astype(BF16)
+            kv_back(i + 1).wait_recv()
+            ov[:, cols] = (dva[h] + sin[i + 1].astype(F32)).astype(BF16)
         outs[1].start()
         outs[2].start()
 
@@ -546,70 +633,132 @@
             (r0f[n] + rin[0, n].astype(F32)) * (0.5 * SCALE)
         ).astype(BF16)
 
-    stages = (
-        (st_q_own, -AHEAD),
-        (st_d_own, SD),
-        (st_q_fwd, 0),
-        (st_d_fwd, SFD),
-        (st_g, LG),
-        (st_c, SC),
-        (st_forward, LF),
-        (st_backward, SB),
-        (st_h, LH),
-        (st_e, SE),
-    )
-    after = {
-        5: [d_gated],
-        LH + 7: [functools.partial(norm, 0)],
-        LH + 15: [functools.partial(norm, 1), weight_terms, outs[3].start],
-        LH + 18: [after_core],
-        LH + 23: [after_two],
-        LH + 27: [after_three, keys_out],
-        SE + 15: [after_four],
-    }
+    def st_forward_mid(n):
+        q_own(n).wait_recv()
+        if n < HEADS:
+            kv_own(2 * (n - MID)).wait_recv()
+            kv_own(2 * (n - MID) + 1).wait_recv()
+        forward_mid(n)
+
+    def st_backward_mid(n):
+        d_own(n).wait_recv()
+        backward_mid(n)
+
+    def once(fn):
+        return lambda _: fn()
+
+    events = []
+
+    def at(time, fn, n=None):
+        events.append((time, fn, n))
+
+    for i in range(2 * (HEADS - MID)):
+        at(-AHEAD - 0.1, once(kv_own(i).start))
+    at(-0.01, once(tables))
+    at(T_GATED, once(d_gated))
+    first = 0
+    for r in range(2):
+        base = r * PER
+        for h in range(MID):
+            n, t = r * HEADS + h, base + h
+            at(t - AHEAD, st_q_own, n)
+            at(t, st_q_fwd, n)
+            at(t + T_OWN, forward_own, n)
+            at(t + HOP, st_forward, n)
+            at(t + 2 * HOP, st_g, n)
+            at(t + 3 * HOP, st_h, n)
+        for i in range(HEADS - MID):
+            n, t = r * HEADS + MID + i, base + MID + 0.5 * i
+            at(t - AHEAD, st_q_own, n)
+            at(t + T_OWN, forward_own, n)
+            at(t + MIDLAG, st_forward_mid, n)
+            at(t + MIDLAG + HOP, st_h, n)
+        last_h = max(time for time, fn, n in events if fn is st_h)
+        at(last_h + 0.01, once(functools.partial(norm, r)))
+        first = max(DM + r * PER, math.ceil(last_h + D_LAG), first + PER)
+        shift = 0 if r == 0 else 1
+        for h in range(MID):
+            n, t = r * HEADS + h, first + shift + h
+            at(max(t - AHEAD, last_h + 0.02), st_d_own, n)
+            at(t, st_d_fwd, n)
+            at(t + HOP, st_backward, n)
+            at(t + 2 * HOP, st_c, n)
+            at(t + 3 * HOP, st_e, n)
+        for i in range(HEADS - MID):
+            n = r * HEADS + MID + i
+            t = first + (MID if r == 0 else 0) + 0.5 * i
+            at(max(t - AHEAD, last_h + 0.02), st_d_own, n)
+            at(t + MIDLAG, st_backward_mid, n)
+            at(t + MIDLAG + HOP, st_e, n)
+    end = first + PER
+    at(last_h + 0.5, once(weight_terms))
+    at(last_h + 0.6, once(outs[3].start))
+    at(last_h + T_CORE, once(after_core))
+    at(last_h + T_TWO, once(after_two))
+    at(last_h + T_THREE, once(after_three))
+    at(last_h + T_FOUR, once(after_four))
+    at(end + T_MID, once(mid_out))
+    at(end + HOP, once(keys_out))
+    at(end + 2 * HOP + 0.5, once(mid_in))
+
+    slots = {}
+    for time, fn, n in sorted(events, key=lambda e: e[0]):
+        slots.setdefault(math.floor(time), []).append((fn, n))
+    order = sorted(slots)
+
+    def steps_of(s):
+        return [(fn, None if n is None else n - s) for fn, n in slots[s]]
+
+    dka[...] = jnp.zeros_like(dka)
+    dva[...] = jnp.zeros_like(dva)
+    dkl[...] = jnp.zeros_like(dkl)
+    dvl[...] = jnp.zeros_like(dvl)
 
     loads[0].wait()
-    pl.semaphore_wait(barrier, len(peers))
-    for n in range(AHEAD):
-        q_own(n).start()
-    tables()
     loads[1].wait()
     loads[2].wait()
-    dka[...] = jnp.zeros_like(dka)
-    dva[...] = jnp.zeros_like(dva)
-
-    last = SE + NCH
-
-    def active(s):
-        return tuple(0 <= s - at < NCH for _, at in stages)
-
-    s = 0
-    while s < last:
-        e = s + 1
-        while e < last and active(e) == active(s) and (e - 1) not in after:
-            e += 1
-        todo = [stage for stage, on in zip(stages, active(s)) if on]
-
-        def slot(i, carry, todo=todo):
-            for fn, at in todo:
-                fn(i - at)
+    pl.semaphore_wait(barrier, len(peers))
+    i = 0
+    while i < len(order):
+        s = order[i]
+        steps = steps_of(s)
+        j = i + 1
+        while (
+            j < len(order)
+            and order[j] == s + (j - i)
+            and steps_of(order[j]) == steps
+            and all(n is not None for _, n in steps)
+        ):
+            j += 1
+
+        def slot(at_slot, carry, steps=steps):
+            for fn, n in steps:
+                fn(None if n is None else at_slot + n)
             return carry
 
-        if e - s == 1:
+        if j - i == 1:
             slot(s, 0)
         else:
-            lax.fori_loop(s, e, slot, 0)
-        for fn in after.get(e - 1, ()):
-            fn()
-        s = e
+            lax.fori_loop(s, s + (j - i), slot, 0)
+        i = j
     outs[0].start()
 
     def drain(n, carry):
-        for copy in (q_own, q_fwd, p_two, p_one, d_own, d_fwd, r_two, r_one):
+        for copy in (q_own, p_one, d_own, r_one):
             copy(n).wait_send()
         return carry
 
+    def drain_two(h, carry):
+        for r in range(2):
+            for copy in (q_fwd, p_two, d_fwd, r_two):
+                copy(r * HEADS + h).wait_send()
+        return carry
+
     lax.fori_loop(0, NCH, drain, 0)
+    lax.fori_loop(0, MID, drain_two, 0)
+    for i in range(2 * (HEADS - MID)):
+        kv_own(i).wait_send()
+        kv_back(i).wait_send()
     if nc > 1:
         for x in range(nx):
             core_copy(x).wait_send()
@@ -625,12 +774,42 @@
         out.wait()
 
 
+def settle(n, *refs):
+    srcs, dsts = refs[:n], refs[n : 2 * n]
+    bufs, isem, osem = refs[2 * n : 3 * n], refs[3 * n], refs[3 * n + 1]
+    ins = [pltpu.make_async_copy(s, b, isem.at[i]) for i, (s, b) in enumerate(zip(srcs, bufs))]
+    outs = [pltpu.make_async_copy(b, d, osem.at[i]) for i, (b, d) in enumerate(zip(bufs, dsts))]
+    for copy in ins:
+        copy.start()
+    for copy, out in zip(ins, outs):
+        copy.wait()
+        out.start()
+    for out in outs:
+        out.wait()
+
+
+def settled(arrays):
+    n = len(arrays)
+    anyspec = pl.BlockSpec(memory_space=pl.ANY)
+    shapes = tuple(jax.ShapeDtypeStruct(a.shape, a.dtype) for a in arrays)
+    return pl.pallas_call(
+        functools.partial(settle, n),
+        out_shape=shapes,
+        in_specs=[anyspec] * n,
+        out_specs=[anyspec] * n,
+        scratch_shapes=[pltpu.VMEM(a.shape, a.dtype) for a in arrays]
+        + [pltpu.SemaphoreType.DMA((n,))] * 2,
+        compiler_params=pltpu.CompilerParams(vmem_limit_bytes=60 * 1024 * 1024),
+    )(*arrays)
+
+
 def on_device(q, k, v, g, c, w, pb, db, hl, fd):
     n_dp = lax.axis_size("dp")
     n_ctx = lax.axis_size("ctx")
     nx, ny, nc = grid = GRIDS[n_dp]
     rw = 1024 // n_dp
     chunk = (NCH, HALF, HD)
+    mids = HEADS - MID
     vm = pltpu.VMEM
     dma = pltpu.SemaphoreType.DMA
     big = jax.ShapeDtypeStruct((1, ROWS, HEADS * HD), BF16)
@@ -638,7 +817,7 @@
     vmem = pl.BlockSpec(memory_space=pltpu.VMEM)
     smem = pl.BlockSpec(memory_space=pltpu.SMEM)
     wide = vm((ROWS, HEADS * HD), BF16)
-    return pl.pallas_call(
+    grads = pl.pallas_call(
         functools.partial(kernel, grid, n_ctx),
         out_shape=(big, big, big, big, jax.ShapeDtypeStruct((rw, HD), F32)),
         in_specs=[anyspec] * 6 + [vmem, vmem, smem, smem],
@@ -671,6 +850,12 @@
             vm((2,) + chunk, BF16),
             vm((HEADS, ROWS, HD), F32),
             vm((HEADS, ROWS, HD), F32),
+            vm((mids, ROWS, HD), BF16),
+            vm((mids, ROWS, HD), BF16),
+            vm((mids, ROWS, HD), F32),
+            vm((mids, ROWS, HD), F32),
+            vm((2 * mids, ROWS, HD), BF16),
+            vm((2 * mids, ROWS, HD), BF16),
             wide,
             wide,
             wide,
@@ -690,12 +875,14 @@
             dma((4,)),
         ]
         + [dma((2, NCH))] * 8
+        + [dma((2 * mids,))] * 4
         + [dma((4,))] * 10
         + [dma((8,))] * 2,
         compiler_params=pltpu.CompilerParams(
             collective_id=0, has_side_effects=True, vmem_limit_bytes=60 * 1024 * 1024
         ),
     )(q, k, v, g, c, w, pb, db, hl, fd)
+    return settled(grads)
 
 
 def solution(mesh):

time: 92.8 us -> 76.2 us (0.82)
  Pallas kernels: 84.3 us -> 74.4 us
  local copies, waits for them, and re-layouts: 6.02 us -> 0 us
    pallas_call x1, Pallas kernels: 84.3 us -> 72 us  [on_device(): pl.pallas_call(functools.partial(kernel, grid, n_ctx), out_shape=(big, bi...]
    unnamed x11 -> x0, local copies, waits for them, and re-layouts: 6.02 us -> none
    pallas_call x0 -> x1, Pallas kernels: none -> 2.44 us  [settled(): pl.pallas_call(functools.partial(settle, n), out_shape=shapes, in_specs=[...]
where the time goes in v2:
time: 76.2 us; the launch traced here: 75.9 us
  Pallas kernels  74.4 us (98%)
  between operations  1.45 us (2%)
    pallas_call x1, Pallas kernels, on_device(): pl.pallas_call(functools.partial(kernel, grid, n_ctx), out_shape=(big, bi...  72 us
    pallas_call x1, Pallas kernels, settled(): pl.pallas_call(functools.partial(settle, n), out_shape=shapes, in_specs=[...  2.44 us

profile of v2, /device:TPU:32, one launch (start us, length us, event | category | flops | bytes accessed | tf_op | source)
XLA Modules:
  0.0 75.9 jit_solution(3955677381526839359)
XLA Ops:
  1.3 72.0 %shard_map.137 = (bf16[1,256,1024]{2,1,0:T(8,128)(2,1)}, bf16[1,256,1024]{2,1,0:T(8,128)(2,1)}, bf16[1,256,1024]{2,1,0:T(8,128)(2,1)}, bf16[1,256,1024]{2,1,0:T(8,128)(2,1)}, f32[32,128]{1,0:T(8,128)}) custom-call(bf16[1,256,1024]{2,1,0:T(8,128)(2,1)} %q_hbm.1, bf16[1,256,1024]{2,1,0:T(8,128)(2,1)} %k_hbm.1, bf16[1,256,1024]{2,1,0:T(8,128)(2,1)} %v_hbm.1, ...), custom_call_target="tpu_custom_call" | custom-call | tf_op jit(solution)/shard_map/pallas_call | solution.py:820
  73.3 2.4 %shard_map.138 = (bf16[1,256,1024]{2,1,0:T(8,128)(2,1)}, bf16[1,256,1024]{2,1,0:T(8,128)(2,1)}, bf16[1,256,1024]{2,1,0:T(8,128)(2,1)}, bf16[1,256,1024]{2,1,0:T(8,128)(2,1)}, f32[32,128]{1,0:T(8,128)}) custom-call(bf16[1,256,1024]{2,1,0:T(8,128)(2,1)} %get-tuple-element.10.refs_0_, bf16[1,256,1024]{2,1,0:T(8,128)(2,1)} %get-tuple-element.11.refs_1_, ...), custom_call_target="tpu_custom_call" | custom-call | tf_op jit(solution)/shard_map/pallas_call | solution.py:795

commit v3 on v2

--- a/solution.py
+++ b/solution.py
@@ -20,12 +20,13 @@
 SCALE = HD ** (-0.5)
 GRIDS = {32: (4, 4, 2), 8: (2, 2, 2), 4: (1, 2, 2), 2: (1, 1, 2), 1: (1, 1, 1)}
 
-MID = 6
-PER = 7
+MID = 5
+MIDS = HEADS - MID
+PAIRED = MID - MIDS
+PER = MID
 
 AHEAD = 4.0
-HOP = 3.5
-MIDLAG = 0.4
+HOP = 3.2
 T_OWN = 0.2
 T_GATED = 8.95
 D_LAG = 1.0
@@ -33,8 +34,6 @@
 T_TWO = 8.0
 T_THREE = 11.5
 T_FOUR = 14.5
-T_MID = 0.4
-DM = 2 * PER
 
 
 def dot_nn(a, b):
@@ -100,6 +99,8 @@
     dvl,
     sout,
     sin,
+    qmux,
+    dmux,
     oq,
     ok,
     ov,
@@ -206,7 +207,10 @@
         (inner + 1 < user_blocks).astype(jnp.int32).astype(F32),
         (inner + 2 < user_blocks).astype(jnp.int32).astype(F32),
     ]
-    valid_mid = ((inner >= 1) & (inner + 1 < user_blocks)).astype(jnp.int32).astype(F32)
+    second = (inner == 1).astype(jnp.int32).astype(F32)
+    third = (inner == 2).astype(jnp.int32).astype(F32)
+    not_third = 1.0 - third
+    middle = ((inner == 1) & (user_blocks == 3)).astype(jnp.int32).astype(F32)
 
     def remote(src, dst, ssem, rsem, device):
         return pltpu.make_async_remote_copy(
@@ -237,6 +241,15 @@
 
     def q_fwd(n):
         return remote(qin.at[0, n], qin.at[1, n], qs.at[1, n], qr.at[1, n], left)
+
+    def mux_at(n):
+        return half_of(n) * MIDS + head_of(n) - PAIRED
+
+    def q_fwd_paired(n):
+        return remote(qmux.at[mux_at(n)], qin.at[1, n], qs.at[1, n], qr.at[1, n], left)
+
+    def d_fwd_paired(n):
+        return remote(dmux.at[mux_at(n)], dmin.at[1, n], ds_.at[1, n], dr.at[1, n], left)
 
     def p_two(n):
         return remote(pout.at[1, n], pin.at[1, n], ps.at[1, n], pr.at[1, n], right)
@@ -321,86 +334,87 @@
         dsav[0, n] = jnp.where(col <= row, d, 0.0)
         mx[n] = dot_nn(a, v0[:, cols_of(n)])
 
-    def forward(n):
+    def attend(qc, kh, vh, h, r, o, slot, n):
+        a, d = curve(qc, kh, h, r, o)
+        a = a.astype(BF16)
+        asav[slot, n] = a
+        dsav[slot, n] = d
+        return dot_nn(a, vh)
+
+    def forward(n, paired=False):
         r, h = half_of(n), head_of(n)
         kh, vh = k0[:, cols_of(n)], v0[:, cols_of(n)]
-        for o in (2, 1):
-            a, d = curve(qin[o - 1, n], kh, h, r, o)
-            a = a.astype(BF16)
-            asav[o, n] = a
-            dsav[o, n] = d
-            part = dot_nn(a, vh) * valid[o]
-            if o == 2:
-                pout[1, n] = part.astype(BF16)
-                p_two(n).start()
-            else:
-                p1f[n] = part
-
-    def forward_mid(n):
-        r, h = half_of(n), head_of(n)
-        total = None
-        for o in (1, 2):
-            kh = k0[:, cols_of(n)] if o == 1 else kl[h - MID]
-            vh = v0[:, cols_of(n)] if o == 1 else vl[h - MID]
-            a, d = curve(qin[0, n], kh, h, r, o)
-            a = a.astype(BF16)
-            asav[o, n] = a
-            dsav[o, n] = d
-            part = dot_nn(a, vh) * (valid[1] if o == 1 else valid_mid)
-            total = part if total is None else total + part
-        pout[0, n] = total.astype(BF16)
-        p_one(n).start()
+        two = attend(qin[1, n], kh, vh, h, r, 2, 2, n) * valid[2]
+        if paired:
+            m, hm, i = n + MIDS, h + MIDS, h - PAIRED
+            km, vm = k0[:, cols_of(m)], v0[:, cols_of(m)]
+            kb, vb = kl[i], vl[i]
+            after = attend(qin[1, n], km, vm, hm, r, 1, 1, m)
+            after = after + attend(qin[1, n], kb, vb, hm, r, 2, 2, m)
+            two = two + after * middle
+        pout[1, n] = two.astype(BF16)
+        p_two(n).start()
+        p1f[n] = attend(qin[0, n], kh, vh, h, r, 1, 1, n) * valid[1]
+        if paired:
+            mx[m] += attend(q0[rows_of(m), cols_of(m)], kb, vb, hm, r, 1, 3, m) * second
 
     def masked(x, flag):
         return (x.astype(F32) * flag).astype(BF16)
 
-    def backward(n):
+    def pull(dmc, kh, vh, slot, n):
+        dsc = (dot_nt(dmc, vh) * dsav[slot, n]).astype(BF16)
+        return dsc, dot_nn(dsc, kh)
+
+    def backward(n, paired=False):
         h = head_of(n)
         kh, vh = k0[:, cols_of(n)], v0[:, cols_of(n)]
-        dss, dms = [], []
-        for o in (2, 1, 0):
-            dmc = dm0[n] if o == 0 else masked(dmin[o - 1, n], valid[o])
-            dsc = (dot_nt(dmc, vh) * dsav[o, n]).astype(BF16)
-            part = dot_nn(dsc, kh)
-            if o == 2:
-                rout[1, n] = part.astype(BF16)
-                r_two(n).start()
-            elif o == 1:
-                r1f[n] = part
-            else:
-                r0f[n] = part
-            dss.append(dsc)
-            dms.append(dmc)
-        qs3 = jnp.concatenate([qin[1, n], qin[0, n], q0[rows_of(n), cols_of(n)]], axis=0)
-        dka[h] += dot_tn(jnp.concatenate(dss, axis=0), qs3)
-        as3 = jnp.concatenate([asav[2, n], asav[1, n], asav[0, n]], axis=0)
-        dva[h] += dot_tn(as3, jnp.concatenate(dms, axis=0))
-
-    def backward_mid(n):
-        h = head_of(n)
-        i = h - MID
-        kh, vh = k0[:, cols_of(n)], v0[:, cols_of(n)]
-        near, far = masked(dmin[0, n], valid[1]), masked(dmin[0, n], valid_mid)
-        ds_far = (dot_nt(far, vl[i]) * dsav[2, n]).astype(BF16)
-        ds_near = (dot_nt(near, vh) * dsav[1, n]).astype(BF16)
-        rout[0, n] = (dot_nn(ds_near, kh) + dot_nn(ds_far, kl[i])).astype(BF16)
-        r_one(n).start()
-        ds_own = (dot_nt(dm0[n], vh) * dsav[0, n]).astype(BF16)
-        r0f[n] = dot_nn(ds_own, kh)
-        qn = qin[0, n]
+        dm_two = masked(dmin[1, n], valid[2])
+        ds_two, part = pull(dm_two, kh, vh, 2, n)
+        if paired:
+            m, hm, i = n + MIDS, h + MIDS, h - PAIRED
+            km, vm = k0[:, cols_of(m)], v0[:, cols_of(m)]
+            kb, vb = kl[i], vl[i]
+            dm_mid = masked(dmin[1, n], middle)
+            ds_near, near = pull(dm_mid, km, vm, 1, m)
+            ds_far, far = pull(dm_mid, kb, vb, 2, m)
+            part = part + near + far
+        rout[1, n] = part.astype(BF16)
+        r_two(n).start()
+        dm_one = masked(dmin[0, n], valid[1])
+        ds_one, r1f[n] = pull(dm_one, kh, vh, 1, n)
+        ds_own, r0f[n] = pull(dm0[n], kh, vh, 0, n)
+        q_own_rows = q0[rows_of(n), cols_of(n)]
         dka[h] += dot_tn(
-            jnp.concatenate([ds_near, ds_own], axis=0),
-            jnp.concatenate([qn, q0[rows_of(n), cols_of(n)]], axis=0),
+            jnp.concatenate([ds_two, ds_one, ds_own], axis=0),
+            jnp.concatenate([qin[1, n], qin[0, n], q_own_rows], axis=0),
         )
         dva[h] += dot_tn(
-            jnp.concatenate([asav[1, n], asav[0, n]], axis=0),
-            jnp.concatenate([near, dm0[n]], axis=0),
-        )
-        dkl[i] += dot_tn(ds_far, qn)
-        dvl[i] += dot_tn(asav[2, n], far)
+            jnp.concatenate([asav[2, n], asav[1, n], asav[0, n]], axis=0),
+            jnp.concatenate([dm_two, dm_one, dm0[n]], axis=0),
+        )
+        if paired:
+            qm, qa = q0[rows_of(m), cols_of(m)], qin[1, n]
+            dm_back = masked(dm0[m], second)
+            ds_back, back = pull(dm_back, kb, vb, 3, m)
+            ds_self, own = pull(dm0[m], km, vm, 0, m)
+            r0f[m] = own + back
+            dka[hm] += dot_tn(
+                jnp.concatenate([ds_near, ds_self], axis=0), jnp.concatenate([qa, qm], axis=0)
+            )
+            dva[hm] += dot_tn(
+                jnp.concatenate([asav[1, m], asav[0, m]], axis=0),
+                jnp.concatenate([dm_mid, dm0[m]], axis=0),
+            )
+            dkl[i] += dot_tn(
+                jnp.concatenate([ds_far, ds_back], axis=0), jnp.concatenate([qa, qm], axis=0)
+            )
+            dvl[i] += dot_tn(
+                jnp.concatenate([asav[2, m], asav[3, m]], axis=0),
+                jnp.concatenate([dm_mid, dm_back], axis=0),
+            )
 
     def mid_out():
-        for i in range(HEADS - MID):
+        for i in range(MIDS):
             sout[2 * i] = (dkl[i] * (0.5 * SCALE)).astype(BF16)
             sout[2 * i + 1] = dvl[i].astype(BF16)
             kv_back(2 * i).start()
@@ -633,16 +647,46 @@
             (r0f[n] + rin[0, n].astype(F32)) * (0.5 * SCALE)
         ).astype(BF16)
 
-    def st_forward_mid(n):
+    def either(mine, passing):
+        return (mine.astype(F32) * third + passing.astype(F32) * not_third).astype(BF16)
+
+    def st_q_fwd_paired(n):
+        m = n + MIDS
         q_own(n).wait_recv()
-        if n < HEADS:
-            kv_own(2 * (n - MID)).wait_recv()
-            kv_own(2 * (n - MID) + 1).wait_recv()
-        forward_mid(n)
-
-    def st_backward_mid(n):
+        qmux[mux_at(n)] = either(q0[rows_of(m), cols_of(m)], qin[0, n])
+        q_fwd_paired(n).start()
+
+    def st_d_fwd_paired(n):
         d_own(n).wait_recv()
-        backward_mid(n)
+        dmux[mux_at(n)] = either(dm0[n + MIDS], dmin[0, n])
+        d_fwd_paired(n).start()
+
+    def st_forward_paired(n):
+        q_fwd(n).wait_recv()
+        forward(n, True)
+
+    def st_backward_paired(n):
+        d_fwd(n).wait_recv()
+        backward(n, True)
+
+    def st_g_paired(n):
+        p_two(n).wait_recv()
+        got = pin[1, n].astype(F32)
+        pout[0, n] = (p1f[n] + got * second).astype(BF16)
+        p_one(n).start()
+        mx[n + MIDS] += got * third
+
+    def st_c_paired(n):
+        r_two(n).wait_recv()
+        got = rin[1, n].astype(F32)
+        rout[0, n] = (r1f[n] + got * second).astype(BF16)
+        r_one(n).start()
+        m = n + MIDS
+        oq[rows_of(m), cols_of(m)] = ((r0f[m] + got * third) * (0.5 * SCALE)).astype(BF16)
+
+    def kv_wait(i):
+        kv_own(2 * i).wait_recv()
+        kv_own(2 * i + 1).wait_recv()
 
     def once(fn):
         return lambda _: fn()
@@ -652,7 +696,7 @@
     def at(time, fn, n=None):
         events.append((time, fn, n))
 
-    for i in range(2 * (HEADS - MID)):
+    for i in range(2 * MIDS):
         at(-AHEAD - 0.1, once(kv_own(i).start))
     at(-0.01, once(tables))
     at(T_GATED, once(d_gated))
@@ -660,36 +704,27 @@
     for r in range(2):
         base = r * PER
         for h in range(MID):
-            n, t = r * HEADS + h, base + h
+            n, t, paired = r * HEADS + h, base + h, h >= PAIRED
             at(t - AHEAD, st_q_own, n)
-            at(t, st_q_fwd, n)
+            at(t, st_q_fwd_paired if paired else st_q_fwd, n)
             at(t + T_OWN, forward_own, n)
-            at(t + HOP, st_forward, n)
-            at(t + 2 * HOP, st_g, n)
+            if paired:
+                at(t + T_OWN, forward_own, n + MIDS)
+                if r == 0:
+                    at(t + HOP - 0.01, once(functools.partial(kv_wait, h - PAIRED)))
+            at(t + HOP, st_forward_paired if paired else st_forward, n)
+            at(t + 2 * HOP, st_g_paired if paired else st_g, n)
             at(t + 3 * HOP, st_h, n)
-        for i in range(HEADS - MID):
-            n, t = r * HEADS + MID + i, base + MID + 0.5 * i
-            at(t - AHEAD, st_q_own, n)
-            at(t + T_OWN, forward_own, n)
-            at(t + MIDLAG, st_forward_mid, n)
-            at(t + MIDLAG + HOP, st_h, n)
         last_h = max(time for time, fn, n in events if fn is st_h)
         at(last_h + 0.01, once(functools.partial(norm, r)))
-        first = max(DM + r * PER, math.ceil(last_h + D_LAG), first + PER)
-        shift = 0 if r == 0 else 1
+        first = max(2 * PER + r * PER, math.ceil(last_h + D_LAG), first + PER)
         for h in range(MID):
-            n, t = r * HEADS + h, first + shift + h
+            n, t, paired = r * HEADS + h, first + h, h >= PAIRED
             at(max(t - AHEAD, last_h + 0.02), st_d_own, n)
-            at(t, st_d_fwd, n)
-            at(t + HOP, st_backward, n)
-            at(t + 2 * HOP, st_c, n)
+            at(t, st_d_fwd_paired if paired else st_d_fwd, n)
+            at(t + HOP, st_backward_paired if paired else st_backward, n)
+            at(t + 2 * HOP, st_c_paired if paired else st_c, n)
             at(t + 3 * HOP, st_e, n)
-        for i in range(HEADS - MID):
-            n = r * HEADS + MID + i
-            t = first + (MID if r == 0 else 0) + 0.5 * i
-            at(max(t - AHEAD, last_h + 0.02), st_d_own, n)
-            at(t + MIDLAG, st_backward_mid, n)
-            at(t + MIDLAG + HOP, st_e, n)
     end = first + PER
     at(last_h + 0.5, once(weight_terms))
     at(last_h + 0.6, once(outs[3].start))
@@ -697,9 +732,9 @@
     at(last_h + T_TWO, once(after_two))
     at(last_h + T_THREE, once(after_three))
     at(last_h + T_FOUR, once(after_four))
-    at(end + T_MID, once(mid_out))
-    at(end + HOP, once(keys_out))
-    at(end + 2 * HOP + 0.5, once(mid_in))
+    at(end - 1 + HOP + 0.02, once(mid_out))
+    at(end - 1 + HOP + 0.03, once(keys_out))
+    at(end - 1 + 3 * HOP + 0.1, once(mid_in))
 
     slots = {}
     for time, fn, n in sorted(events, key=lambda e: e[0]):
@@ -743,20 +778,15 @@
         i = j
     outs[0].start()
 
-    def drain(n, carry):
-        for copy in (q_own, p_one, d_own, r_one):
-            copy(n).wait_send()
+    def drain(h, carry):
+        for r in range(2):
+            n = r * HEADS + h
+            for copy in (q_own, q_fwd, p_two, p_one, d_own, d_fwd, r_two, r_one):
+                copy(n).wait_send()
         return carry
 
-    def drain_two(h, carry):
-        for r in range(2):
-            for copy in (q_fwd, p_two, d_fwd, r_two):
-                copy(r * HEADS + h).wait_send()
-        return carry
-
-    lax.fori_loop(0, NCH, drain, 0)
-    lax.fori_loop(0, MID, drain_two, 0)
-    for i in range(2 * (HEADS - MID)):
+    lax.fori_loop(0, MID, drain, 0)
+    for i in range(2 * MIDS):
         kv_own(i).wait_send()
         kv_back(i).wait_send()
     if nc > 1:
@@ -809,7 +839,6 @@
     nx, ny, nc = grid = GRIDS[n_dp]
     rw = 1024 // n_dp
     chunk = (NCH, HALF, HD)
-    mids = HEADS - MID
     vm = pltpu.VMEM
     dma = pltpu.SemaphoreType.DMA
     big = jax.ShapeDtypeStruct((1, ROWS, HEADS * HD), BF16)
@@ -837,8 +866,8 @@
             vm(chunk, F32),
             vm((2,) + chunk, BF16),
             vm((2,) + chunk, BF16),
-            vm((3, NCH, HALF, ROWS), BF16),
-            vm((3, NCH, HALF, ROWS), F32),
+            vm((4, NCH, HALF, ROWS), BF16),
+            vm((4, NCH, HALF, ROWS), F32),
             vm(chunk, F32),
             vm(chunk, F32),
             wide,
@@ -850,12 +879,14 @@
             vm((2,) + chunk, BF16),
             vm((HEADS, ROWS, HD), F32),
             vm((HEADS, ROWS, HD), F32),
-            vm((mids, ROWS, HD), BF16),
-            vm((mids, ROWS, HD), BF16),
-            vm((mids, ROWS, HD), F32),
-            vm((mids, ROWS, HD), F32),
-            vm((2 * mids, ROWS, HD), BF16),
-            vm((2 * mids, ROWS, HD), BF16),
+            vm((MIDS, ROWS, HD), BF16),
+            vm((MIDS, ROWS, HD), BF16),
+            vm((MIDS, ROWS, HD), F32),
+            vm((MIDS, ROWS, HD), F32),
+            vm((2 * MIDS, ROWS, HD), BF16),
+            vm((2 * MIDS, ROWS, HD), BF16),
+            vm((2 * MIDS, HALF, HD), BF16),
+            vm((2 * MIDS, HALF, HD), BF16),
             wide,
             wide,
             wide,
@@ -875,7 +906,7 @@
             dma((4,)),
         ]
         + [dma((2, NCH))] * 8
-        + [dma((2 * mids,))] * 4
+        + [dma((2 * MIDS,))] * 4
         + [dma((4,))] * 10
         + [dma((8,))] * 2,
         compiler_params=pltpu.CompilerParams(

time: 76.2 us -> 70.7 us (0.928)
  Pallas kernels: 74.4 us -> 69.1 us
    pallas_call x1, Pallas kernels: 72 us -> 66.6 us  [on_device(): pl.pallas_call(functools.partial(kernel, grid, n_ctx), out_shape=(big, bi...]
where the time goes in v3:
time: 70.7 us; the launch traced here: 70.5 us
  Pallas kernels  69.1 us (98%)
  between operations  1.45 us (2%)
    pallas_call x1, Pallas kernels, on_device(): pl.pallas_call(functools.partial(kernel, grid, n_ctx), out_shape=(big, bi...  66.6 us
    pallas_call x1, Pallas kernels, settled(): pl.pallas_call(functools.partial(settle, n), out_shape=shapes, in_specs=[...  2.44 us

profile of v3, /device:TPU:32, one launch (start us, length us, event | category | flops | bytes accessed | tf_op | source)
XLA Modules:
  0.0 70.5 jit_solution(10452003112002140474)
XLA Ops:
  1.3 66.6 %shard_map.137 = (bf16[1,256,1024]{2,1,0:T(8,128)(2,1)}, bf16[1,256,1024]{2,1,0:T(8,128)(2,1)}, bf16[1,256,1024]{2,1,0:T(8,128)(2,1)}, bf16[1,256,1024]{2,1,0:T(8,128)(2,1)}, f32[32,128]{1,0:T(8,128)}) custom-call(bf16[1,256,1024]{2,1,0:T(8,128)(2,1)} %q_hbm.1, bf16[1,256,1024]{2,1,0:T(8,128)(2,1)} %k_hbm.1, bf16[1,256,1024]{2,1,0:T(8,128)(2,1)} %v_hbm.1, ...), custom_call_target="tpu_custom_call" | custom-call | tf_op jit(solution)/shard_map/pallas_call | solution.py:849
  67.9 2.4 %shard_map.138 = (bf16[1,256,1024]{2,1,0:T(8,128)(2,1)}, bf16[1,256,1024]{2,1,0:T(8,128)(2,1)}, bf16[1,256,1024]{2,1,0:T(8,128)(2,1)}, bf16[1,256,1024]{2,1,0:T(8,128)(2,1)}, f32[32,128]{1,0:T(8,128)}) custom-call(bf16[1,256,1024]{2,1,0:T(8,128)(2,1)} %get-tuple-element.10.refs_0_, bf16[1,256,1024]{2,1,0:T(8,128)(2,1)} %get-tuple-element.11.refs_1_, ...), custom_call_target="tpu_custom_call" | custom-call | tf_op jit(solution)/shard_map/pallas_call | solution.py:825

commit v4 on v3

--- a/solution.py
+++ b/solution.py
@@ -20,7 +20,7 @@
 SCALE = HD ** (-0.5)
 GRIDS = {32: (4, 4, 2), 8: (2, 2, 2), 4: (1, 2, 2), 2: (1, 1, 2), 1: (1, 1, 1)}
 
-MID = 5
+MID = 4
 MIDS = HEADS - MID
 PAIRED = MID - MIDS
 PER = MID
@@ -142,6 +142,7 @@
     b3r,
     fs,
     fr,
+    tell,
 ):
     nx, ny, nc = grid
     dp = lax.axis_index("dp")
@@ -162,9 +163,9 @@
         return (x * (ny * nc) + y * nc + c, ctx)
 
     other = 1 - ci
-    peers = [(dp, lax.rem(ctx + k, n_ctx)) for k in range(1, n_ctx)]
-    peers += [dev(at_x(k), yi, ci) for k in range(1, nx)]
-    peers += [dev(xi, at_y(k), ci) for k in range(1, ny)]
+    peers = [(dp, lax.rem(ctx + k, n_ctx)) for k in sorted({1, n_ctx - 1})]
+    peers += [dev(at_x(k), yi, ci) for k in sorted({1, nx - 1} - {0})]
+    peers += [dev(xi, at_y(k), ci) for k in sorted({1, ny - 1} - {0})]
     if nc > 1:
         peers.append(dev(xi, yi, other))
 
@@ -413,12 +414,11 @@
                 jnp.concatenate([dm_mid, dm_back], axis=0),
             )
 
-    def mid_out():
-        for i in range(MIDS):
-            sout[2 * i] = (dkl[i] * (0.5 * SCALE)).astype(BF16)
-            sout[2 * i + 1] = dvl[i].astype(BF16)
-            kv_back(2 * i).start()
-            kv_back(2 * i + 1).start()
+    def mid_out(i):
+        sout[2 * i] = (dkl[i] * (0.5 * SCALE)).astype(BF16)
+        sout[2 * i + 1] = dvl[i].astype(BF16)
+        kv_back(2 * i).start()
+        kv_back(2 * i + 1).start()
 
     def live_mask(r, width):
         row = lax.broadcasted_iota(jnp.int32, (HALF, width), 0) + r * HALF
@@ -530,6 +530,10 @@
                     if nc > 1:
                         got = got + cin[x, y, half].astype(F32)
                     c1[x, y, half] = got.astype(BF16)
+        if nx == 4:
+            pl.semaphore_wait(tell.at[0], 1)
+        if ny == 4:
+            pl.semaphore_wait(tell.at[1], 1)
         for k in range(1, nx):
             a_copy(k).start()
         for k in range(1, ny):
@@ -718,8 +722,13 @@
         last_h = max(time for time, fn, n in events if fn is st_h)
         at(last_h + 0.01, once(functools.partial(norm, r)))
         first = max(2 * PER + r * PER, math.ceil(last_h + D_LAG), first + PER)
-        for h in range(MID):
-            n, t, paired = r * HEADS + h, first + h, h >= PAIRED
+        turn = list(range(MID))
+        if r == 1:
+            turn = turn[PAIRED:] + turn[:PAIRED]
+        for place, h in enumerate(turn):
+            n, t, paired = r * HEADS + h, first + place, h >= PAIRED
+            if r == 1 and paired:
+                at(t + HOP + 0.02, once(functools.partial(mid_out, h - PAIRED)))
             at(max(t - AHEAD, last_h + 0.02), st_d_own, n)
             at(t, st_d_fwd_paired if paired else st_d_fwd, n)
             at(t + HOP, st_backward_paired if paired else st_backward, n)
@@ -732,7 +741,6 @@
     at(last_h + T_TWO, once(after_two))
     at(last_h + T_THREE, once(after_three))
     at(last_h + T_FOUR, once(after_four))
-    at(end - 1 + HOP + 0.02, once(mid_out))
     at(end - 1 + HOP + 0.03, once(keys_out))
     at(end - 1 + 3 * HOP + 0.1, once(mid_in))
 
@@ -753,6 +761,10 @@
     loads[1].wait()
     loads[2].wait()
     pl.semaphore_wait(barrier, len(peers))
+    if nx == 4:
+        pl.semaphore_signal(tell.at[0], inc=1, device_id=dev(at_x(3), yi, ci), device_id_type=MESH)
+    if ny == 4:
+        pl.semaphore_signal(tell.at[1], inc=1, device_id=dev(xi, at_y(3), ci), device_id_type=MESH)
     i = 0
     while i < len(order):
         s = order[i]
@@ -908,7 +920,8 @@
         + [dma((2, NCH))] * 8
         + [dma((2 * MIDS,))] * 4
         + [dma((4,))] * 10
-        + [dma((8,))] * 2,
+        + [dma((8,))] * 2
+        + [pltpu.SemaphoreType.REGULAR((2,))],
         compiler_params=pltpu.CompilerParams(
             collective_id=0, has_side_effects=True, vmem_limit_bytes=60 * 1024 * 1024
         ),

time: 70.7 us -> 66.8 us (0.945)
  Pallas kernels: 69.1 us -> 65.2 us
    pallas_call x1, Pallas kernels: 66.6 us -> 62.7 us  [on_device(): pl.pallas_call(functools.partial(kernel, grid, n_ctx), out_shape=(big, bi...]
where the time goes in v4:
time: 66.8 us; the launch traced here: 66.6 us
  Pallas kernels  65.2 us (98%)
  between operations  1.45 us (2%)
    pallas_call x1, Pallas kernels, on_device(): pl.pallas_call(functools.partial(kernel, grid, n_ctx), out_shape=(big, bi...  62.7 us
    pallas_call x1, Pallas kernels, settled(): pl.pallas_call(functools.partial(settle, n), out_shape=shapes, in_specs=[...  2.44 us

profile of v4, /device:TPU:32, one launch (start us, length us, event | category | flops | bytes accessed | tf_op | source)
XLA Modules:
  0.0 66.6 jit_solution(2656356896376747439)
XLA Ops:
  1.3 62.7 %shard_map.137 = (bf16[1,256,1024]{2,1,0:T(8,128)(2,1)}, bf16[1,256,1024]{2,1,0:T(8,128)(2,1)}, bf16[1,256,1024]{2,1,0:T(8,128)(2,1)}, bf16[1,256,1024]{2,1,0:T(8,128)(2,1)}, f32[32,128]{1,0:T(8,128)}) custom-call(bf16[1,256,1024]{2,1,0:T(8,128)(2,1)} %q_hbm.1, bf16[1,256,1024]{2,1,0:T(8,128)(2,1)} %k_hbm.1, bf16[1,256,1024]{2,1,0:T(8,128)(2,1)} %v_hbm.1, ...), custom_call_target="tpu_custom_call" | custom-call | tf_op jit(solution)/shard_map/pallas_call | solution.py:861
  64.0 2.4 %shard_map.138 = (bf16[1,256,1024]{2,1,0:T(8,128)(2,1)}, bf16[1,256,1024]{2,1,0:T(8,128)(2,1)}, bf16[1,256,1024]{2,1,0:T(8,128)(2,1)}, bf16[1,256,1024]{2,1,0:T(8,128)(2,1)}, f32[32,128]{1,0:T(8,128)}) custom-call(bf16[1,256,1024]{2,1,0:T(8,128)(2,1)} %get-tuple-element.10.refs_0_, bf16[1,256,1024]{2,1,0:T(8,128)(2,1)} %get-tuple-element.11.refs_1_, ...), custom_call_target="tpu_custom_call" | custom-call | tf_op jit(solution)/shard_map/pallas_call | solution.py:837

commit v5 on v4

--- a/solution.py
+++ b/solution.py
@@ -29,11 +29,11 @@
 HOP = 3.2
 T_OWN = 0.2
 T_GATED = 8.95
-D_LAG = 1.0
+D_LAG = 1.6
 T_CORE = 3.0
 T_TWO = 8.0
-T_THREE = 11.5
-T_FOUR = 14.5
+T_THREE = 10.6
+T_FOUR = 13.6
 
 
 def dot_nn(a, b):
@@ -701,7 +701,7 @@
         events.append((time, fn, n))
 
     for i in range(2 * MIDS):
-        at(-AHEAD - 0.1, once(kv_own(i).start))
+        at(max(-AHEAD - 0.1, i // 2 * 2.0 - 3.95), once(kv_own(i).start))
     at(-0.01, once(tables))
     at(T_GATED, once(d_gated))
     first = 0

time: 66.8 us -> 66.4 us (level)
  no operation moved by 1% of the time
where the time goes in v5:
time: 66.4 us; the launch traced here: 66.2 us
  Pallas kernels  64.8 us (98%)
  between operations  1.45 us (2%)
    pallas_call x1, Pallas kernels, on_device(): pl.pallas_call(functools.partial(kernel, grid, n_ctx), out_shape=(big, bi...  62.4 us
    pallas_call x1, Pallas kernels, settled(): pl.pallas_call(functools.partial(settle, n), out_shape=shapes, in_specs=[...  2.44 us

profile of v5, /device:TPU:32, one launch (start us, length us, event | category | flops | bytes accessed | tf_op | source)
XLA Modules:
  0.0 66.2 jit_solution(17464904514337020993)
XLA Ops:
  1.3 62.4 %shard_map.137 = (bf16[1,256,1024]{2,1,0:T(8,128)(2,1)}, bf16[1,256,1024]{2,1,0:T(8,128)(2,1)}, bf16[1,256,1024]{2,1,0:T(8,128)(2,1)}, bf16[1,256,1024]{2,1,0:T(8,128)(2,1)}, f32[32,128]{1,0:T(8,128)}) custom-call(bf16[1,256,1024]{2,1,0:T(8,128)(2,1)} %q_hbm.1, bf16[1,256,1024]{2,1,0:T(8,128)(2,1)} %k_hbm.1, bf16[1,256,1024]{2,1,0:T(8,128)(2,1)} %v_hbm.1, ...), custom_call_target="tpu_custom_call" | custom-call | tf_op jit(solution)/shard_map/pallas_call | solution.py:861
  63.6 2.4 %shard_map.138 = (bf16[1,256,1024]{2,1,0:T(8,128)(2,1)}, bf16[1,256,1024]{2,1,0:T(8,128)(2,1)}, bf16[1,256,1024]{2,1,0:T(8,128)(2,1)}, bf16[1,256,1024]{2,1,0:T(8,128)(2,1)}, f32[32,128]{1,0:T(8,128)}) custom-call(bf16[1,256,1024]{2,1,0:T(8,128)(2,1)} %get-tuple-element.10.refs_0_, bf16[1,256,1024]{2,1,0:T(8,128)(2,1)} %get-tuple-element.11.refs_1_, ...), custom_call_target="tpu_custom_call" | custom-call | tf_op jit(solution)/shard_map/pallas_call | solution.py:837
